TPU v7x, 32 devices: a whole 2x2x4 slice. The times are simulated.
32 devices in a mesh: gx: 8 (over z, core), gy: 4 (over y, x).
Axes of the slice: x: 2, y: 2, z: 4, core: 2. Of those that a mesh axis runs over, the one named last changes fastest.
Arguments:
- offset: float32 [3, 768, 128], P(None, ('gx', 'gy')), may hold values from 0.5 to 1.5
- particle_mass: float32 [768, 128], P(('gx', 'gy')), may hold values from 0.5 to 2
- velocity: float32 [3, 768, 128], P(None, ('gx', 'gy')), may hold values from -6 to 6
- affine: float32 [9, 768, 128], P(None, ('gx', 'gy')), may hold values from -3 to 3
- deform: float32 [9, 768, 128], P(None, ('gx', 'gy')), may hold values from -0.3 to 1.3, as said below
- particle_cell: int32 [768, 128], P(('gx', 'gy')), may hold values from 0 to 127
- body_id: int32 [768, 128], P(('gx', 'gy')), may hold values from 0 to 63
- slot_tile_number: int32 [768], P(('gx', 'gy')), may hold values from 0 to 127, as said below
- block_count: int32 [8, 4], P('gx', 'gy'), may hold values from 12 to 24, as said below
- normal_code: int32 [64, 32, 256], P('gx', 'gy'), may hold values from 0 to 25
Outputs:
- new_velocity: float32 [3, 768, 128], P(None, ('gx', 'gy'))
- new_affine: float32 [9, 768, 128], P(None, ('gx', 'gy'))
- new_deform: float32 [9, 768, 128], P(None, ('gx', 'gy'))
- new_stress: float32 [6, 768, 128], P(None, ('gx', 'gy'))
Inputs may be any that keep to these rules, and one draw needn't show every extreme that they name: `deform`: A 3 x 3 identity plus entries between -0.3 and 0.3. `slot_tile_number`: on every device the first four slots lie in tiles on the low x, high x, low y and high y faces of its part of the grid, in that order. `block_count`: slots below the count are live; some device has exactly 24.
All inputs are finite; a program needn't handle non-finite values.
Results may differ from a plain program's by a relative error of at most 0.000073.
Values sent between devices are 32-bit elements; how exact they have to be, the bound alone decides.
A program may use at most 128 MiB of HBM per device.

v0:
```python
import jax
import jax.numpy as jnp
from jax import lax
from jax.sharding import PartitionSpec as P

DT = 0.1
MU = 2.0
LAM = 3.0
GRAVITY = -2.0
FLOOR = 0.25


def from_behind(block, axis, distance):
    devices = range(lax.axis_size(axis))
    route = [(i - distance, i) for i in devices if i - distance in devices]
    return lax.ppermute(block, axis, route)


def padded(block, sides, width):
    for axis, dim in sides:
        count = lax.axis_size(axis)
        forward = [(i, i + 1) for i in range(count - 1)]
        backward = [(target, source) for source, target in forward]
        low = lax.ppermute(
            lax.slice_in_dim(block, block.shape[dim] - width, None, axis=dim), axis, forward
        )
        high = lax.ppermute(lax.slice_in_dim(block, 0, width, axis=dim), axis, backward)
        block = jnp.concatenate([low, block, high], axis=dim)
    return block


def spline_weights(fraction):
    return [
        0.5 * (1.5 - fraction) * (1.5 - fraction),
        0.75 - (fraction - 1.0) * (fraction - 1.0),
        0.5 * (fraction - 0.5) * (fraction - 0.5),
    ]


def determinant(matrix):
    return (
        matrix[0] * (matrix[4] * matrix[8] - matrix[5] * matrix[7])
        - matrix[1] * (matrix[3] * matrix[8] - matrix[5] * matrix[6])
        + matrix[2] * (matrix[3] * matrix[7] - matrix[4] * matrix[6])
    )


def kirchhoff(matrix):
    volume_ratio = determinant(matrix)
    pressure = 0.5 * LAM * (volume_ratio * volume_ratio - 1.0)
    entries = []
    for row_index in range(3):
        for column_position in range(3):
            element = (
                matrix[3 * row_index] * matrix[3 * column_position]
                + matrix[3 * row_index + 1] * matrix[3 * column_position + 1]
                + matrix[3 * row_index + 2] * matrix[3 * column_position + 2]
            )
            if row_index == column_position:
                element = MU * (element - 1.0) + pressure
            else:
                element = MU * element
            entries.append(element)
    return jnp.stack(entries)


def advance_deform(affine_new, deform):
    entries = []
    for row_index in range(3):
        for column_position in range(3):
            element = deform[3 * row_index + column_position]
            for inner_index in range(3):
                element = (
                    element
                    + DT
                    * affine_new[3 * row_index + inner_index]
                    * deform[3 * inner_index + column_position]
                )
            entries.append(element)
    return jnp.stack(entries)


def unit_normals(direction):
    shifted = direction + (direction >= 13).astype(jnp.int32)
    components = [shifted // 9 - 1, shifted // 3 % 3 - 1, shifted % 3 - 1]
    components = [part_value.astype(jnp.float32) for part_value in components]
    length = jnp.sqrt(
        components[0] * components[0]
        + components[1] * components[1]
        + components[2] * components[2]
    )
    return jnp.stack([part_value / length for part_value in components])


def node_update(node_grid, normal):
    first_body_mass = node_grid[0]
    momentum_zero = node_grid[1:4]
    mass_one = node_grid[4]
    momentum_one = node_grid[5:8]
    gravity_step = jnp.array([0.0, 0.0, DT * GRAVITY], dtype=node_grid.dtype).reshape(
        (3,) + (1,) * (node_grid.ndim - 1)
    )
    speed_zero = momentum_zero / jnp.maximum(first_body_mass, FLOOR) + gravity_step
    speed_one = momentum_one / jnp.maximum(mass_one, FLOOR) + gravity_step
    center_speed = (momentum_zero + momentum_one) / jnp.maximum(
        first_body_mass + mass_one, FLOOR
    ) + gravity_step
    contact_share = jnp.minimum(1.0, jnp.minimum(first_body_mass, mass_one) / FLOOR)
    approach_zero = jnp.maximum(jnp.sum((speed_zero - center_speed) * normal, 0), 0.0)
    approach_one = jnp.maximum(jnp.sum((center_speed - speed_one) * normal, 0), 0.0)
    speed_zero = speed_zero - (contact_share * approach_zero)[None] * normal
    speed_one = speed_one + (contact_share * approach_one)[None] * normal
    return jnp.concatenate([speed_zero, speed_one], 0)


def patch_axis(fraction, cell_coord, node_coord):
    weights = spline_weights(fraction)
    weight_sum = jnp.zeros(fraction.shape + node_coord.shape, jnp.float32)
    moment_sum = jnp.zeros(fraction.shape + node_coord.shape, jnp.float32)
    for stencil in range(3):
        onehot = (cell_coord[..., None] + stencil == node_coord).astype(jnp.float32)
        weight_sum = weight_sum + weights[stencil][..., None] * onehot
        moment_sum = moment_sum + (weights[stencil] * (stencil - fraction))[..., None] * onehot
    return (weight_sum, moment_sum)


def build_weights(fraction, cell_index, column_x, column_y, column_z):
    weight_x, moment_x = patch_axis(fraction[0], cell_index // 32, column_x)
    weight_y, moment_y = patch_axis(fraction[1], cell_index // 8 % 4, column_y)
    weight_z, moment_z = patch_axis(fraction[2], cell_index % 8, column_z)
    shared_yz = weight_y * weight_z
    return jnp.stack(
        [
            weight_x * shared_yz,
            moment_x * shared_yz,
            weight_x * moment_y * weight_z,
            weight_x * weight_y * moment_z,
        ],
        1,
    )


def per_device(
    offset,
    particle_mass,
    velocity,
    affine,
    deform,
    particle_cell,
    body_id,
    slot_tile_number,
    block_count,
    normal_code,
):
    blocks, particles = particle_mass.shape
    side_x, vertical_extent, depth_z = normal_code.shape
    vertical_tiles = vertical_extent // 4
    tiles_z = depth_z // 8
    group_size = 8
    groups = blocks // group_size
    live_count = block_count[0, 0]
    live_mask = (jnp.arange(blocks, dtype=jnp.int32) < live_count).astype(jnp.float32)[:, None]
    field_zero = (body_id % 2 == 0).astype(jnp.float32)
    field_one = 1.0 - field_zero
    weighted = particle_mass * live_mask
    stress_old = kirchhoff(deform)
    affine_force = weighted[None] * (affine - 4.0 * DT * stress_old)
    zero_rows = jnp.zeros_like(weighted)
    channel_sets = [
        [weighted * field_zero]
        + [weighted * velocity[row_index] * field_zero for row_index in range(3)]
        + [weighted * field_one]
        + [weighted * velocity[row_index] * field_one for row_index in range(3)]
    ]
    for column_position in range(3):
        channel_sets.append(
            [zero_rows]
            + [affine_force[3 * row_index + column_position] * field_zero for row_index in range(3)]
            + [zero_rows]
            + [affine_force[3 * row_index + column_position] * field_one for row_index in range(3)]
        )
    sources = jnp.stack([jnp.stack(channels) for channels in channel_sets])
    column = jnp.arange(384, dtype=jnp.int32)
    column_x = column // 60
    column_y = column // 10 % 6
    column_z = column % 10

    def scatter_work(members):
        fraction, cell_index, source = members
        kernel = build_weights(fraction, cell_index, column_x, column_y, column_z)
        return jnp.einsum("lcgp,glpq->cgq", source, kernel, precision=lax.Precision.HIGHEST)

    def scatter_step(group_index, patches):
        start = group_index * group_size
        fraction = lax.dynamic_slice_in_dim(offset, start, group_size, 1)
        cell_index = lax.dynamic_slice_in_dim(particle_cell, start, group_size, 0)
        source = lax.dynamic_slice_in_dim(sources, start, group_size, 2)
        result = scatter_work((fraction, cell_index, source))
        return lax.dynamic_update_slice_in_dim(patches, result, start, 1)

    patches = lax.fori_loop(0, groups, scatter_step, jnp.zeros((8, blocks, 384), jnp.float32))
    tile_x = slot_tile_number // (vertical_tiles * tiles_z)
    tile_y = slot_tile_number // tiles_z % vertical_tiles
    tile_z = slot_tile_number % tiles_z
    grid_cells = (side_x + 2) * (vertical_extent + 2) * (depth_z + 2)
    node_x = tile_x[:, None] * 4 + column_x[None, :]
    node_y = tile_y[:, None] * 4 + column_y[None, :]
    node_z = tile_z[:, None] * 8 + column_z[None, :]
    flat_index = (node_x * (vertical_extent + 2) + node_y) * (depth_z + 2) + node_z
    flat_index = jnp.where(column[None, :] < 360, flat_index, grid_cells)
    node_grid = jnp.zeros((8, grid_cells + 1), jnp.float32)
    node_grid = node_grid.at[:, flat_index].add(patches)
    node_grid = node_grid[:, :grid_cells].reshape(8, side_x + 2, vertical_extent + 2, depth_z + 2)
    depth_index = jnp.arange(depth_z + 2, dtype=jnp.int32)
    inside_z = ((depth_index >= 1) & (depth_index <= depth_z)).astype(jnp.float32)
    from_right = from_behind(node_grid[:, 0:1], "gx", -1)
    from_left = from_behind(node_grid[:, side_x + 1 : side_x + 2], "gx", 1)
    inner_rows = node_grid[:, 1 : side_x + 1]
    inner_rows = inner_rows.at[:, side_x - 1 : side_x].add(from_right).at[:, 0:1].add(from_left)
    from_above = from_behind(inner_rows[:, :, 0:1], "gy", -1)
    from_below = from_behind(inner_rows[:, :, vertical_extent + 1 : vertical_extent + 2], "gy", 1)
    inner_rows = (
        inner_rows.at[:, :, vertical_extent : vertical_extent + 1]
        .add(from_above)
        .at[:, :, 1:2]
        .add(from_below)
    )
    owned_nodes = inner_rows[:, :, 1 : vertical_extent + 1]
    normal = jnp.pad(unit_normals(normal_code), ((0, 0), (0, 0), (0, 0), (1, 1)))
    speeds = node_update(owned_nodes, normal) * inside_z
    speeds = padded(speeds, (("gx", 1), ("gy", 2)), 1)
    flat_speeds = jnp.concatenate([speeds.reshape(6, -1), jnp.zeros((6, 1), jnp.float32)], 1)
    block_speeds = flat_speeds[:, flat_index]

    def gather_work(members):
        fraction, cell_index, speed_rows = members
        kernel = build_weights(fraction, cell_index, column_x, column_y, column_z)
        return jnp.einsum("glpq,cgq->lcgp", kernel, speed_rows, precision=lax.Precision.HIGHEST)

    def gather_step(group_index, gathered):
        start = group_index * group_size
        fraction = lax.dynamic_slice_in_dim(offset, start, group_size, 1)
        cell_index = lax.dynamic_slice_in_dim(particle_cell, start, group_size, 0)
        speed_rows = lax.dynamic_slice_in_dim(block_speeds, start, group_size, 1)
        result = gather_work((fraction, cell_index, speed_rows))
        return lax.dynamic_update_slice_in_dim(gathered, result, start, 2)

    gathered = lax.fori_loop(
        0, groups, gather_step, jnp.zeros((4, 6, blocks, particles), jnp.float32)
    )
    chosen = gathered[:, 0:3] * field_zero + gathered[:, 3:6] * field_one
    new_velocity = chosen[0] * live_mask
    new_affine = (
        4.0
        * jnp.stack(
            [
                chosen[1 + column_position][row_index]
                for row_index in range(3)
                for column_position in range(3)
            ]
        )
        * live_mask
    )
    new_deform = advance_deform(new_affine, deform) * live_mask
    stress_new = kirchhoff(new_deform)
    new_stress = (
        jnp.stack(
            [
                stress_new[0],
                stress_new[4],
                stress_new[8],
                stress_new[1],
                stress_new[2],
                stress_new[5],
            ]
        )
        * live_mask
    )
    return (new_velocity, new_affine, new_deform, new_stress)


def solution(mesh):
    placed = (
        P(None, ("gx", "gy"), None),
        P(("gx", "gy"), None),
        P(None, ("gx", "gy"), None),
        P(None, ("gx", "gy"), None),
        P(None, ("gx", "gy"), None),
        P(("gx", "gy"), None),
        P(("gx", "gy"), None),
        P(("gx", "gy")),
        P("gx", "gy"),
        P("gx", "gy", None),
    )
    return jax.shard_map(
        per_device,
        mesh=mesh,
        in_specs=placed,
        out_specs=(
            P(None, ("gx", "gy"), None),
            P(None, ("gx", "gy"), None),
            P(None, ("gx", "gy"), None),
            P(None, ("gx", "gy"), None),
        ),
        check_vma=False,
    )
```

profile of v0, /device:TPU:13, one launch (start us, length us, event | category | flops | bytes accessed | tf_op | source)
XLA Modules:
  0.0 284.6 jit_solution(620609627112127170)
XLA Ops:
  13.0 42.8 %while.40 = (s32[]{:T(128)}, f32[8,24,384]{2,0,1:T(8,128)S(1)}, s32[24,128]{1,0:T(8,128)S(1)}, f32[3,24,128]{2,1,0:T(8,128)S(1)}, f32[4,8,24,128]{3,2,1,0:T(8,12...) while((s32[]{:T(128)}, f32[8,24,384]{2,0,1:T(8,128)S(1)}, ...), condition=%wide.region_1.2_spmd.clone.clone, body=%wide.region_0.1_spmd.clone.clone.sunk | while | flops 196723456 | bytes 13550299 | solution.py:201
  13.2 2.7 fusion.162
  15.9 2.7 fusion.163
  18.5 2.7 fusion.164
  21.2 2.7 fusion.161
  23.9 3.4 %fusion.165 = f32[8,24,384]{2,0,1:T(8,128)S(1)} fusion(f32[8,24,384]{2,0,1:T(8,128)S(1)} %get-tuple-element.1021, s32[]{:T(128)S(6)} %select_n.500, f32[8,1,128,384]{3,2,1,0:T(8,128)S(1)} %fusion.161, f32[8,1,128,384]{3,2,1,0:T(8,128)S(1)} %fusion.162, f32[8,1,128,384]{3,2,1,0:T(8,128)S(1)} %fusion.163, f32[8,1,128,384]{3,2,1,0:T(8,128)S(1)} %fusion.164, ...), kind=kOutput, calls=%fused_computation.54.clone.1 | convolution fusion | flops 155713536 | bytes 6520836 | tf_op jit(solution)/shard_map/while/body/eval_jaxpr/lcgp,glpq->cgq/dot_general | solution.py:191
  27.5 2.7 fusion.162
  30.1 2.7 fusion.163
  32.8 2.7 fusion.164
  35.5 2.7 fusion.161
  38.2 3.4 %fusion.165 = f32[8,24,384]{2,0,1:T(8,128)S(1)} fusion(f32[8,24,384]{2,0,1:T(8,128)S(1)} %get-tuple-element.1021, s32[]{:T(128)S(6)} %select_n.500, f32[8,1,128,384]{3,2,1,0:T(8,128)S(1)} %fusion.161, f32[8,1,128,384]{3,2,1,0:T(8,128)S(1)} %fusion.162, f32[8,1,128,384]{3,2,1,0:T(8,128)S(1)} %fusion.163, f32[8,1,128,384]{3,2,1,0:T(8,128)S(1)} %fusion.164, ...), kind=kOutput, calls=%fused_computation.54.clone.1 | convolution fusion | flops 155713536 | bytes 6520836 | tf_op jit(solution)/shard_map/while/body/eval_jaxpr/lcgp,glpq->cgq/dot_general | solution.py:191
  41.7 2.7 fusion.162
  44.4 2.7 fusion.163
  47.1 2.7 fusion.164
  49.8 2.7 fusion.161
  52.5 3.4 %fusion.165 = f32[8,24,384]{2,0,1:T(8,128)S(1)} fusion(f32[8,24,384]{2,0,1:T(8,128)S(1)} %get-tuple-element.1021, s32[]{:T(128)S(6)} %select_n.500, f32[8,1,128,384]{3,2,1,0:T(8,128)S(1)} %fusion.161, f32[8,1,128,384]{3,2,1,0:T(8,128)S(1)} %fusion.162, f32[8,1,128,384]{3,2,1,0:T(8,128)S(1)} %fusion.163, f32[8,1,128,384]{3,2,1,0:T(8,128)S(1)} %fusion.164, ...), kind=kOutput, calls=%fused_computation.54.clone.1 | convolution fusion | flops 155713536 | bytes 6520836 | tf_op jit(solution)/shard_map/while/body/eval_jaxpr/lcgp,glpq->cgq/dot_general | solution.py:191
  55.9 2.8 %copy.25 = f32[9216,8]{1,0:T(8,128)} copy(f32[9216,8]{0,1:T(8,128)S(1)} %bitcast.343) | data formatting | bytes 589824 | tf_op jit(solution)/shard_map/while | solution.py:201
  58.8 55.9 %scatter_custom_fusion = f32[8,25801]{0,1:T(8,128)} fusion(s32[9216]{0:T(1024)S(1)} %reshape.1325, f32[9216,8]{1,0:T(8,128)} %copy.25, f32[]{:T(128)} %constant.860.clone.1), kind=kCustom, calls=%fused_computation.225 | custom fusion | flops 73728 | bytes 826144 | tf_op jit(solution)/shard_map/scatter-add | solution.py:212
  114.8 9.6 %slice.697 = f32[8,25800]{0,1:T(8,128)} slice(f32[8,25801]{0,1:T(8,128)} %scatter_custom_fusion), slice={[0:8], [0:25800]} | slice | bytes 1651200 | tf_op jit(solution)/shard_map/slice | solution.py:213
  124.3 8.1 %copy.26 = f32[8,25800]{1,0:T(8,128)S(1)} copy(f32[8,25800]{0,1:T(8,128)} %slice.697) | data formatting | bytes 1651200 | tf_op jit(solution)/shard_map/slice | solution.py:213
  133.5 2.6 collective-permute-start
  136.1 3.1 %collective-permute-start.1 = (f32[8,1,10,258]{3,2,1,0:T(8,128)S(1)}, f32[8,1,10,258]{3,2,1,0:T(8,128)S(1)}, u32[]{:S(2)}, u32[]{:S(2)}) collective-permute-start(f32[8,1,10,258]{3,2,1,0:T(8,128)S(1)} %get-tuple-element.788), channel_id=1, source_target_pairs={{0,4},{4,8},{8,12},{12,16},{16,20},{20,24},{24,28},{1,5},{5,9},{9,... | collective-permute-start | bytes 247688 | tf_op jit(solution)/shard_map/ppermute | solution.py:16
  142.0 3.1 %collective-permute-start.2 = (f32[8,8,1,258]{3,2,1,0:T(1,128)S(1)}, f32[8,8,1,258]{3,2,1,0:T(1,128)S(1)}, u32[]{:S(2)}, u32[]{:S(2)}) collective-permute-start(f32[8,8,1,258]{3,2,1,0:T(1,128)S(1)} %get-tuple-element.798), channel_id=1, source_target_pairs={{1,0},{2,1},{3,2},{5,4},{6,5},{7,6},{9,8},{10,9},{11,10},{13,12},{... | collective-permute-start | bytes 198152 | tf_op jit(solution)/shard_map/ppermute | solution.py:16
  147.5 3.5 %scatter-add.30 = f32[8,8,10,258]{3,2,1,0:T(8,128)S(1)} dynamic-update-slice(f32[8,8,10,258]{3,2,1,0:T(8,128)S(1)} %fusion.106, f32[8,8,1,258]{3,2,1,0:T(1,128)S(1)} %slice_add_fusion.3, s32[]{:T(128)} %constant.859.clone.1, s32[]{:T(128)} %constant.859.clone.1, s32[]{:T(128)} %constant.874.clone.1, s32[]{:T(128)} %constant.859.clone.1) | dynamic-update-slice | bytes 132100 | tf_op jit(solution)/shard_map/scatter-add | solution.py:224
  151.5 3.5 %scatter-add.31 = f32[8,8,10,258]{3,2,1,0:T(8,128)S(1)} dynamic-update-slice(f32[8,8,10,258]{3,2,1,0:T(8,128)S(1)} %scatter-add.30, f32[8,8,1,258]{3,2,1,0:T(1,128)S(1)} %slice_add_fusion.2, s32[]{:T(128)} %constant.859.clone.1, s32[]{:T(128)} %constant.859.clone.1, s32[]{:T(128)} %constant.862.clone.1, s32[]{:T(128)} %constant.859.clone.1) | dynamic-update-slice | bytes 132100 | tf_op jit(solution)/shard_map/scatter-add | solution.py:226
  156.6 5.8 %collective-permute-start.4 = (f32[6,1,8,258]{3,2,1,0:T(8,128)S(1)}, f32[6,1,8,258]{3,2,1,0:T(8,128)S(1)}, u32[]{:S(2)}, u32[]{:S(2)}) collective-permute-start(f32[6,1,8,258]{3,2,1,0:T(8,128)S(1)} %get-tuple-element.801), channel_id=1, source_target_pairs={{0,4},{4,8},{8,12},{12,16},{16,20},{20,24},{24,28},{1,5},{5,9},{9,... | collective-permute-start | bytes 148616 | tf_op jit(solution)/shard_map/ppermute | solution.py:24
  164.3 3.7 %collective-permute-done.5 = f32[6,1,8,258]{3,2,1,0:T(8,128)S(1)} collective-permute-done((f32[6,1,8,258]{3,2,1,0:T(8,128)S(1)}, f32[6,1,8,258]{3,2,1,0:T(8,128)S(1)}, u32[]{:S(2)}, u32[]{:S(2)}) %collective-permute-start.5) | collective-permute-done | bytes 49568 | tf_op jit(solution)/shard_map/ppermute | solution.py:27
  170.1 4.3 %collective-permute-start.7 = (f32[6,10,1,258]{3,2,1,0:T(1,128)S(1)}, f32[6,10,1,258]{3,2,1,0:T(1,128)S(1)}, u32[]{:S(2)}, u32[]{:S(2)}) collective-permute-start(f32[6,10,1,258]{3,2,1,0:T(1,128)S(1)} %get-tuple-element.800), channel_id=1, source_target_pairs={{1,0},{2,1},{3,2},{5,4},{6,5},{7,6},{9,8},{10,9},{11,10},{13,12},{... | collective-permute-start | bytes 185768 | tf_op jit(solution)/shard_map/ppermute | solution.py:27
  177.2 7.8 %copy.27 = f32[6,25800]{0,1:T(8,128)} copy(f32[6,25800]{1,0:T(8,128)S(1)} %reshape.1314) | data formatting | bytes 1238400 | tf_op jit(solution)/shard_map/reshape | solution.py:232
  185.1 9.7 %concatenate.23 = f32[6,25801]{0,1:T(8,128)} pad(f32[6,25800]{0,1:T(8,128)} %copy.27, f32[]{:T(128)} %constant.860.clone.1), padding=0_0x0_1 | pad | bytes 1238428 | tf_op jit(solution)/shard_map/concatenate | solution.py:232
  194.8 35.9 %gather_fusion = f32[9216,6]{1,0:T(8,128)} fusion(f32[6,25801]{0,1:T(8,128)} %concatenate.23, s32[9216]{0:T(1024)S(1)} %copy-done.10), kind=kCustom, calls=%fused_computation | custom fusion | bytes 479232 | tf_op jit(solution)/shard_map/gather | solution.py:233
  230.7 3.1 %copy.28 = f32[24,384,6]{1,2,0:T(8,128)S(1)} copy(f32[24,384,6]{2,1,0:T(8,128)} %bitcast.342) | data formatting | bytes 442368 | tf_op jit(solution)/shard_map/gather | solution.py:233
  233.9 48.7 %while.41 = (s32[]{:T(128)}, f32[4,6,24,128]{3,2,1,0:T(8,128)S(1)}, f32[6,24,384]{2,0,1:T(8,128)S(1)}, s32[24,128]{1,0:T(8,128)S(1)}, f32[3,24,128]{2,1,0:T(8,12...) while((s32[]{:T(128)}, f32[4,6,24,128]{3,2,1,0:T(8,128)S(1)}, ...), condition=%wide.region_6.7_spmd.clone.clone, body=%wide.region_5.6_spmd.clone.clone.sunk | while | flops 158974720 | bytes 13484763 | solution.py:248
  234.0 2.7 fusion.169
  236.7 2.7 fusion.170
  239.4 2.7 fusion.171
  242.1 2.7 fusion.168
  244.7 5.3 %fusion.172 = f32[4,6,8,128]{3,1,0,2:T(8,128)S(1)} fusion(f32[8,1,128,384]{3,2,1,0:T(8,128)S(1)} %fusion.168, f32[8,1,128,384]{3,2,1,0:T(8,128)S(1)} %fusion.169, f32[8,1,128,384]{3,2,1,0:T(8,128)S(1)} %fusion.170, f32[8,1,128,384]{3,2,1,0:T(8,128)S(1)} %fusion.171, f32[6,24,384]{2,0,1:T(8,128)S(1)} %get-tuple-element.1066, s32[]{:T(128)S(6)} %select_n.503), kind=kOutput, calls=%fused_computation.161.clone.1 | convolution fusion | flops 117964800 | bytes 6488068 | tf_op jit(solution)/shard_map/while/body/eval_jaxpr/glpq,cgq->lcgp/dot_general | solution.py:238
  250.3 2.7 fusion.169
  253.0 2.7 fusion.170
  255.6 2.7 fusion.171
  258.3 2.7 fusion.168
  261.0 5.3 %fusion.172 = f32[4,6,8,128]{3,1,0,2:T(8,128)S(1)} fusion(f32[8,1,128,384]{3,2,1,0:T(8,128)S(1)} %fusion.168, f32[8,1,128,384]{3,2,1,0:T(8,128)S(1)} %fusion.169, f32[8,1,128,384]{3,2,1,0:T(8,128)S(1)} %fusion.170, f32[8,1,128,384]{3,2,1,0:T(8,128)S(1)} %fusion.171, f32[6,24,384]{2,0,1:T(8,128)S(1)} %get-tuple-element.1066, s32[]{:T(128)S(6)} %select_n.503), kind=kOutput, calls=%fused_computation.161.clone.1 | convolution fusion | flops 117964800 | bytes 6488068 | tf_op jit(solution)/shard_map/while/body/eval_jaxpr/glpq,cgq->lcgp/dot_general | solution.py:238
  266.5 2.7 fusion.169
  269.2 2.7 fusion.170
  271.9 2.7 fusion.171
  274.6 2.7 fusion.168
  277.2 5.3 %fusion.172 = f32[4,6,8,128]{3,1,0,2:T(8,128)S(1)} fusion(f32[8,1,128,384]{3,2,1,0:T(8,128)S(1)} %fusion.168, f32[8,1,128,384]{3,2,1,0:T(8,128)S(1)} %fusion.169, f32[8,1,128,384]{3,2,1,0:T(8,128)S(1)} %fusion.170, f32[8,1,128,384]{3,2,1,0:T(8,128)S(1)} %fusion.171, f32[6,24,384]{2,0,1:T(8,128)S(1)} %get-tuple-element.1066, s32[]{:T(128)S(6)} %select_n.503), kind=kOutput, calls=%fused_computation.161.clone.1 | convolution fusion | flops 117964800 | bytes 6488068 | tf_op jit(solution)/shard_map/while/body/eval_jaxpr/glpq,cgq->lcgp/dot_general | solution.py:238
  (183 shorter events, 29.4 us)
Async XLA Ops:
  0.6 12.4 %copy-start.3 = (f32[3,24,128]{2,1,0:T(8,128)S(1)}, f32[3,24,128]{2,1,0:T(8,128)}, u32[]{:S(2)}) copy-start(f32[3,24,128]{2,1,0:T(8,128)} %param.23) | copy-start | bytes 110596
  0.6 12.4 %copy-start.8 = (s32[24,128]{1,0:T(8,128)S(1)}, s32[24,128]{1,0:T(8,128)}, u32[]{:S(2)}) copy-start(s32[24,128]{1,0:T(8,128)} %param.28) | copy-start | bytes 36868
  6.7 3.0 %copy-start.12 = (f32[24]{0:T(128)}, f32[24]{0:T(128)S(1)}, u32[]{:S(2)}) copy-start(f32[24]{0:T(128)S(1)} %compare_convert_fusion) | copy-start | bytes 292
  55.8 2.9 %copy-start.15 = (s32[24]{0:T(128)S(1)}, s32[24]{0:T(128)}, u32[]{:S(2)}) copy-start(s32[24]{0:T(128)} %param.30) | copy-start | bytes 292
  132.4 7.4 %copy-start.9 = (s32[8,8,256]{2,1,0:T(8,128)S(1)}, s32[8,8,256]{2,1,0:T(8,128)}, u32[]{:S(2)}) copy-start(s32[8,8,256]{2,1,0:T(8,128)} %param.32) | copy-start | bytes 196612
  133.5 8.1 %collective-permute-start = (f32[8,1,10,258]{3,2,1,0:T(8,128)S(1)}, f32[8,1,10,258]{3,2,1,0:T(8,128)S(1)}, u32[]{:S(2)}, u32[]{:S(2)}) collective-permute-start(f32[8,1,10,258]{3,2,1,0:T(8,128)S(1)} %get-tuple-element.789), channel_id=1, source_target_pairs={{4,0},{8,4},{12,8},{16,12},{20,16},{24,20},{28,24},{5,1},{9,5},{13... | collective-permute-start | bytes 247688 | tf_op jit(solution)/shard_map/ppermute | solution.py:16
  136.1 5.7 %collective-permute-start.1 = (f32[8,1,10,258]{3,2,1,0:T(8,128)S(1)}, f32[8,1,10,258]{3,2,1,0:T(8,128)S(1)}, u32[]{:S(2)}, u32[]{:S(2)}) collective-permute-start(f32[8,1,10,258]{3,2,1,0:T(8,128)S(1)} %get-tuple-element.788), channel_id=1, source_target_pairs={{0,4},{4,8},{8,12},{12,16},{16,20},{20,24},{24,28},{1,5},{5,9},{9,... | collective-permute-start | bytes 247688 | tf_op jit(solution)/shard_map/ppermute | solution.py:16
  142.0 5.4 %collective-permute-start.2 = (f32[8,8,1,258]{3,2,1,0:T(1,128)S(1)}, f32[8,8,1,258]{3,2,1,0:T(1,128)S(1)}, u32[]{:S(2)}, u32[]{:S(2)}) collective-permute-start(f32[8,8,1,258]{3,2,1,0:T(1,128)S(1)} %get-tuple-element.798), channel_id=1, source_target_pairs={{1,0},{2,1},{3,2},{5,4},{6,5},{7,6},{9,8},{10,9},{11,10},{13,12},{... | collective-permute-start | bytes 198152 | tf_op jit(solution)/shard_map/ppermute | solution.py:16
  145.1 6.3 %collective-permute-start.3 = (f32[8,8,1,258]{3,2,1,0:T(1,128)S(1)}, f32[8,8,1,258]{3,2,1,0:T(1,128)S(1)}, u32[]{:S(2)}, u32[]{:S(2)}) collective-permute-start(f32[8,8,1,258]{3,2,1,0:T(1,128)S(1)} %get-tuple-element.797), channel_id=1, source_target_pairs={{0,1},{1,2},{2,3},{4,5},{5,6},{6,7},{8,9},{9,10},{10,11},{12,13},{... | collective-permute-start | bytes 198152 | tf_op jit(solution)/shard_map/ppermute | solution.py:16
  147.5 8.8 %copy-start.5 = (f32[1,8,8,256]{3,2,1,0:T(8,128)S(1)}, f32[1,8,8,256]{3,2,1,0:T(8,128)}, u32[]{:S(2)}) copy-start(f32[1,8,8,256]{3,2,1,0:T(8,128)} %get-tuple-element.730) | copy-start | bytes 196612
  147.5 8.8 %copy-start.6 = (f32[1,8,8,256]{3,2,1,0:T(8,128)S(1)}, f32[1,8,8,256]{3,2,1,0:T(8,128)}, u32[]{:S(2)}) copy-start(f32[1,8,8,256]{3,2,1,0:T(8,128)} %get-tuple-element.803) | copy-start | bytes 196612
  147.5 8.8 %copy-start.7 = (f32[1,8,8,256]{3,2,1,0:T(8,128)S(1)}, f32[1,8,8,256]{3,2,1,0:T(8,128)}, u32[]{:S(2)}) copy-start(f32[1,8,8,256]{3,2,1,0:T(8,128)} %get-tuple-element.804) | copy-start | bytes 196612
  147.5 8.8 %copy-start.14 = (f32[3]{0:T(128)S(1)}, f32[3]{0:T(128)}, u32[]{:S(2)}) copy-start(f32[3]{0:T(128)} %constant.890.clone) | copy-start | bytes 40
  156.6 7.8 %collective-permute-start.4 = (f32[6,1,8,258]{3,2,1,0:T(8,128)S(1)}, f32[6,1,8,258]{3,2,1,0:T(8,128)S(1)}, u32[]{:S(2)}, u32[]{:S(2)}) collective-permute-start(f32[6,1,8,258]{3,2,1,0:T(8,128)S(1)} %get-tuple-element.801), channel_id=1, source_target_pairs={{0,4},{4,8},{8,12},{12,16},{16,20},{20,24},{24,28},{1,5},{5,9},{9,... | collective-permute-start | bytes 148616 | tf_op jit(solution)/shard_map/ppermute | solution.py:24
  162.4 5.7 %collective-permute-start.5 = (f32[6,1,8,258]{3,2,1,0:T(8,128)S(1)}, f32[6,1,8,258]{3,2,1,0:T(8,128)S(1)}, u32[]{:S(2)}, u32[]{:S(2)}) collective-permute-start(f32[6,1,8,258]{3,2,1,0:T(8,128)S(1)} %get-tuple-element.802), channel_id=1, source_target_pairs={{4,0},{8,4},{12,8},{16,12},{20,16},{24,20},{28,24},{5,1},{9,5},{13... | collective-permute-start | bytes 148616 | tf_op jit(solution)/shard_map/ppermute | solution.py:27
  168.2 6.4 %collective-permute-start.6 = (f32[6,10,1,258]{3,2,1,0:T(1,128)S(1)}, f32[6,10,1,258]{3,2,1,0:T(1,128)S(1)}, u32[]{:S(2)}, u32[]{:S(2)}) collective-permute-start(f32[6,10,1,258]{3,2,1,0:T(1,128)S(1)} %get-tuple-element.799), channel_id=1, source_target_pairs={{0,1},{1,2},{2,3},{4,5},{5,6},{6,7},{8,9},{9,10},{10,11},{12,13},{... | collective-permute-start | bytes 185768 | tf_op jit(solution)/shard_map/ppermute | solution.py:24
  170.1 6.2 %collective-permute-start.7 = (f32[6,10,1,258]{3,2,1,0:T(1,128)S(1)}, f32[6,10,1,258]{3,2,1,0:T(1,128)S(1)}, u32[]{:S(2)}, u32[]{:S(2)}) collective-permute-start(f32[6,10,1,258]{3,2,1,0:T(1,128)S(1)} %get-tuple-element.800), channel_id=1, source_target_pairs={{1,0},{2,1},{3,2},{5,4},{6,5},{7,6},{9,8},{10,9},{11,10},{13,12},{... | collective-permute-start | bytes 185768 | tf_op jit(solution)/shard_map/ppermute | solution.py:27
  185.1 9.7 %copy-start.10 = (s32[9216]{0:T(1024)S(1)}, s32[9216]{0:T(1024)}, u32[]{:S(2)}) copy-start(s32[9216]{0:T(1024)} %broadcast_clamp_fusion) | copy-start | bytes 110596
  230.7 3.1 %copy-start.4 = (f32[3,24,128]{2,1,0:T(8,128)S(1)}, f32[3,24,128]{2,1,0:T(8,128)}, u32[]{:S(2)}) copy-start(f32[3,24,128]{2,1,0:T(8,128)} %param.23) | copy-start | bytes 110596
  233.8 48.8 %copy-start.11 = (f32[24,128]{1,0:T(8,128)S(1)}, f32[24,128]{1,0:T(8,128)}, u32[]{:S(2)}) copy-start(f32[24,128]{1,0:T(8,128)} %get-tuple-element.728) | copy-start | bytes 36868
  233.8 48.8 %copy-start.13 = (f32[24]{0:T(128)S(1)}, f32[24]{0:T(128)}, u32[]{:S(2)}) copy-start(f32[24]{0:T(128)} %copy-done.12) | copy-start | bytes 292
  233.8 49.7 %copy-start = (f32[9,24,128]{2,1,0:T(8,128)S(1)}, f32[9,24,128]{2,1,0:T(8,128)}, u32[]{:S(2)}) copy-start(f32[9,24,128]{2,1,0:T(8,128)} %param.27) | copy-start | bytes 331780
  283.5 1.1 copy-start.2
  283.8 0.8 copy-start.1
where the time goes:
time: 288 us; the launch traced here: 285 us
  other arithmetic  138 us (48%)
  local copies, waits for them, and re-layouts  86.5 us (30%)
  matrix products  26 us (9%)
  starting transfers between devices  24.9 us (9%)
  waiting for transfers between devices  6.22 us (2%)
    scatter-add x1, other arithmetic, per_device(): node_grid = node_grid.at[:, flat_index].add(patches)  55.9 us
    gather x2, local copies, waits for them, and re-layouts, per_device(): block_speeds = flat_speeds[:, flat_index]  39 us
    slice x2, local copies, waits for them, and re-layouts, per_device(): node_grid[:, :grid_cells]  17.7 us
    mul x6, other arithmetic, build_weights(): weight_x * shared_yz  16 us
    mul x6, other arithmetic, build_weights(): moment_x * shared_yz  16 us
    mul x6, other arithmetic, build_weights(): weight_x * moment_y * weight_z  16 us
    mul x6, other arithmetic, build_weights(): weight_x * weight_y * moment_z  16 us
    dot_general x3, matrix products, gather_work(): jnp.einsum('glpq,cgq->lcgp', kernel, speed_rows, precision=lax.Precision....  15.9 us
  transfers between devices with their start and end apart: 8, of which 5 were waited for; matrix products, arithmetic and copies ran while one was open for 2% of the time, Pallas kernels for 0%

commit v1 on v0

v1 whole, which is shorter than its diff:
```python
import functools

import jax
import jax.numpy as jnp
from jax import lax
from jax.experimental import pallas as pl
from jax.experimental.pallas import tpu as pltpu
from jax.sharding import PartitionSpec as P

DT = 0.1
MU = 2.0
LAM = 3.0
GRAVITY = -2.0
FLOOR = 0.25
LANES = 128
SUB = 8
TILE_X, TILE_Y, TILE_Z = 4, 4, 8
SPAN_Z = TILE_Z + 2
MESH = pl.DeviceIdType.MESH
F32 = jnp.float32
BF16 = jnp.bfloat16
DIRECTIONS = [(-1, 0), (1, 0), (0, -1), (0, 1), (-1, -1), (-1, 1), (1, -1), (1, 1)]


def spline_weights(fraction):
    return [
        0.5 * (1.5 - fraction) * (1.5 - fraction),
        0.75 - (fraction - 1.0) * (fraction - 1.0),
        0.5 * (fraction - 0.5) * (fraction - 0.5),
    ]


def determinant(m):
    return (
        m[0] * (m[4] * m[8] - m[5] * m[7])
        - m[1] * (m[3] * m[8] - m[5] * m[6])
        + m[2] * (m[3] * m[7] - m[4] * m[6])
    )


def kirchhoff(m):
    ratio = determinant(m)
    pressure = 0.5 * LAM * (ratio * ratio - 1.0)

    def dot(r, c):
        return m[3 * r] * m[3 * c] + m[3 * r + 1] * m[3 * c + 1] + m[3 * r + 2] * m[3 * c + 2]

    return [MU * (dot(r, r) - 1.0) + pressure for r in range(3)] + [
        MU * dot(0, 1),
        MU * dot(0, 2),
        MU * dot(1, 2),
    ]


SYMMETRIC = [0, 3, 4, 3, 1, 5, 4, 5, 2]


def split(value):
    high = value.astype(BF16)
    return high, (value - high.astype(F32)).astype(BF16)


def store_rows(rows_ref, blocks, offset_ref, cell_ref):
    cell = cell_ref[...]
    cells = [cell // (TILE_Y * TILE_Z), cell // TILE_Z % TILE_Y, cell % TILE_Z]
    rows = []
    for axis in range(2):
        fraction = offset_ref[axis]
        weights = spline_weights(fraction)
        rows.append(cells[axis].astype(F32))
        rows.extend(weights)
        rows.extend(weights[step] * (step - fraction) for step in range(3))
    fraction = offset_ref[2]
    weights = spline_weights(fraction)
    moments = [weights[step] * (step - fraction) for step in range(3)]
    for values in (weights, moments):
        for k in range(SPAN_Z):
            total = jnp.zeros_like(fraction)
            for step in range(3):
                total = jnp.where(cells[2] == k - step, values[step], total)
            rows.append(total)
    for index, row in enumerate(rows):
        rows_ref[pl.ds(index * blocks, blocks), :] = row


N_ROWS = 14 + 2 * SPAN_Z


def node_coordinates(n_y, padded_nodes):
    node = lax.broadcasted_iota(jnp.int32, (padded_nodes, LANES), 0)
    return (node // n_y).astype(F32), (node % n_y).astype(F32)


def plane_weights(rows_ref, blocks, block, tile, tiles, coordinates):
    tiles_y, tiles_z = tiles
    tile_x = (tile // (tiles_y * tiles_z) * TILE_X).astype(F32)
    tile_y = (tile // tiles_z % tiles_y * TILE_Y).astype(F32)

    def row(index):
        return rows_ref[pl.ds(index * blocks + block, 1), :]

    parts = []
    for axis, corner in enumerate((tile_x, tile_y)):
        first = 7 * axis
        step = coordinates[axis] - (row(first) + corner)
        hits = [step == float(s) for s in range(3)]
        for shift in (1, 4):
            total = jnp.zeros_like(step)
            for s in range(3):
                total = jnp.where(hits[s], row(first + shift + s), total)
            parts.append(total)
    weight_x, moment_x, weight_y, moment_y = parts
    out = [weight_x * weight_y, moment_x * weight_y, weight_x * moment_y]
    pad = jnp.zeros((LANES - coordinates[0].shape[0], LANES), F32)
    return [jnp.concatenate([p, pad], 0) for p in out]


def scatter_kernel(
    shape,
    tile_ref,
    count_ref,
    offset_ref,
    mass_ref,
    velocity_ref,
    affine_ref,
    deform_ref,
    cell_ref,
    body_ref,
    grid_ref,
    source_ref,
    rows_ref,
):
    n_y, padded_nodes, tiles, unroll = shape
    blocks = mass_ref.shape[0]
    slot = lax.broadcasted_iota(jnp.int32, mass_ref.shape, 0)
    mass = jnp.where(slot < count_ref[0, 0], mass_ref[...], 0.0)
    even = body_ref[...] % 2 == 0
    masses = [jnp.where(even, mass, 0.0), jnp.where(even, 0.0, mass)]
    tau = kirchhoff([deform_ref[i] for i in range(9)])
    force = [affine_ref[i] - 4.0 * DT * tau[SYMMETRIC[i]] for i in range(9)]
    zero = jnp.zeros_like(mass)

    def put(group, channel, value):
        source_ref[pl.ds(group * blocks * SUB + channel, blocks, stride=SUB), :] = value

    for field in range(2):
        put(0, 4 * field, masses[field])
        for r in range(3):
            put(0, 4 * field + 1 + r, masses[field] * velocity_ref[r])
        for c in range(3):
            put(1 + c, 4 * field, zero)
            for r in range(3):
                put(1 + c, 4 * field + 1 + r, masses[field] * force[3 * r + c])
    store_rows(rows_ref, blocks, offset_ref, cell_ref)
    grid_ref[...] = jnp.zeros_like(grid_ref)
    coordinates = node_coordinates(n_y, padded_nodes)

    def block_sums(block):
        tile = tile_ref[block]
        planes = plane_weights(rows_ref, blocks, block, tile, tiles, coordinates)
        groups = [
            source_ref[
                pl.ds(pl.multiple_of(g * blocks * SUB + block * SUB, SUB), SUB), :
            ]
            for g in range(4)
        ]
        left = [[], [], []]
        for k in range(SPAN_Z):
            weight = rows_ref[pl.ds((14 + k) * blocks + block, 1), :]
            moment = rows_ref[pl.ds((14 + SPAN_Z + k) * blocks + block, 1), :]
            left[0].append(groups[0] * weight + groups[3] * moment)
            left[1].append(groups[1] * weight)
            left[2].append(groups[2] * weight)
        left = jnp.concatenate([jnp.concatenate(part, 0) for part in left], 1)
        right = jnp.concatenate(planes, 1)
        left_high, left_low = split(left)
        right_high, right_low = split(right)
        product = lax.dot_general(
            jnp.concatenate([left_high, left_low], 0),
            jnp.concatenate([right_high, right_low], 0),
            (((1,), (1,)), ((), ())),
            preferred_element_type=F32,
        )
        n = SPAN_Z * SUB
        return product[:n, :LANES] + (product[:n, LANES:] + product[n:, :LANES])

    def step(index, carry):
        members = [index * unroll + u for u in range(unroll)]
        sums = [block_sums(block) for block in members]
        for block, patch in zip(members, sums):
            start = pl.multiple_of(tile_ref[block] % tiles[1] * (TILE_Z * SUB), SUB)
            window = pl.ds(start, SPAN_Z * SUB)
            grid_ref[window, :] = grid_ref[window, :] + patch
        return carry

    lax.fori_loop(0, blocks // unroll, step, 0)


def face_runs(direction, n_x, n_y):
    dx, dy = direction
    xs = {-1: (0, 2), 0: (0, n_x), 1: (n_x - 2, 2)}[dx]
    ys = {-1: (0, 2), 0: (0, n_y), 1: (n_y - 2, 2)}[dy]
    if dy == 0:
        return [(xs[0] * n_y, xs[1] * n_y)]
    return [((xs[0] + i) * n_y + ys[0], ys[1]) for i in range(xs[1])]


def face_nodes(direction, n_x, n_y):
    return sum(count for _, count in face_runs(direction, n_x, n_y))


def exchange_kernel(shape, grid_ref, code_ref, speed_ref, *scratch):
    n_x, n_y, padded_nodes, halves = shape
    node_ref, codes_ref, planes_ref, send_code, recv_code = scratch[:5]
    sends = scratch[5:13]
    recvs = scratch[13:21]
    send_sem, recv_sem, code_send_sem, code_recv_sem = scratch[21:]
    size_x, size_y = lax.axis_size("gx"), lax.axis_size("gy")
    me_x, me_y = lax.axis_index("gx"), lax.axis_index("gy")
    own_x, own_y = n_x - 2, n_y - 2
    valid = []
    for dx, dy in DIRECTIONS:
        ok = None
        for d, me, size in ((dx, me_x, size_x), (dy, me_y, size_y)):
            if d == 0:
                continue
            one = me > 0 if d < 0 else me < size - 1
            ok = one if ok is None else jnp.logical_and(ok, one)
        valid.append(ok)
    barrier = pltpu.get_barrier_semaphore()

    def target(index):
        dx, dy = DIRECTIONS[index]
        return {"gx": me_x + dx, "gy": me_y + dy}

    for index in range(8):

        @pl.when(valid[index])
        def _(index=index):
            pl.semaphore_signal(
                barrier, inc=1, device_id=target(index), device_id_type=MESH
            )

    opposite = [DIRECTIONS.index((-dx, -dy)) for dx, dy in DIRECTIONS]
    plane = padded_nodes * SUB

    for half in range(halves):
        lanes = pl.ds(half * LANES, LANES)
        rows = pl.ds(half * own_y, own_y)
        for index, (dx, dy) in enumerate(DIRECTIONS):
            x = 0 if dx < 0 else own_x - 1
            y = 0 if dy < 0 else own_y - 1
            if dy == 0:
                send_code[index, rows, :] = code_ref[x, :, lanes]
            elif dx == 0:
                for i in range(own_x):
                    send_code[index, pl.ds(half * own_y + i, 1), :] = code_ref[
                        i, pl.ds(y, 1), lanes
                    ]
            else:
                send_code[index, rows, :] = jnp.broadcast_to(
                    code_ref[x, pl.ds(y, 1), lanes], (own_y, LANES)
                )

    def code_copy(index):
        return pltpu.make_async_remote_copy(
            src_ref=send_code.at[index],
            dst_ref=recv_code.at[opposite[index]],
            send_sem=code_send_sem.at[index],
            recv_sem=code_recv_sem.at[opposite[index]],
            device_id=target(index),
            device_id_type=MESH,
        )

    def face_copy(index):
        return pltpu.make_async_remote_copy(
            src_ref=sends[index],
            dst_ref=recvs[opposite[index]],
            send_sem=send_sem.at[index],
            recv_sem=recv_sem.at[opposite[index]],
            device_id=target(index),
            device_id_type=MESH,
        )

    for half in range(halves):
        for c in range(SUB):
            part = grid_ref[pl.ds((1 + half * LANES) * SUB + c, LANES, stride=SUB), :]
            node_ref[pl.ds(half * plane + c, padded_nodes, stride=SUB), :] = part.T[
                :padded_nodes
            ]

    def each_run(index):
        offset = 0
        for half in range(halves):
            for first, count in face_runs(DIRECTIONS[index], n_x, n_y):
                yield (
                    pl.ds(half * plane + first * SUB, count * SUB),
                    pl.ds(offset, count * SUB),
                )
                offset += count * SUB

    for index in range(8):
        for nodes, run in each_run(index):
            sends[index][run, :] = node_ref[nodes, :]

    arrivals = sum(ok.astype(jnp.int32) for ok in valid)
    pl.semaphore_wait(barrier, arrivals)
    for index in [2, 3, 4, 5, 6, 7, 0, 1]:

        @pl.when(valid[index])
        def _(index=index):
            code_copy(index).start()
            face_copy(index).start()

        @pl.when(jnp.logical_not(valid[index]))
        def _(index=index):
            recv_code[index] = jnp.zeros(recv_code.shape[1:], jnp.int32)
            recvs[index][...] = jnp.zeros_like(recvs[index])

    codes_ref[...] = jnp.zeros_like(codes_ref)
    for half in range(halves):
        lanes = pl.ds(half * LANES, LANES)
        for x in range(own_x):
            codes_ref[pl.ds(half * padded_nodes + (x + 1) * n_y + 1, own_y), :] = code_ref[
                x, :, lanes
            ]
    planes_ref[:, pl.ds(padded_nodes, LANES - padded_nodes), :] = jnp.zeros(
        (planes_ref.shape[0], LANES - padded_nodes, LANES), F32
    )

    for index in [0, 1, 4, 5, 6, 7, 2, 3]:

        @pl.when(valid[index])
        def _(index=index):
            code_copy(opposite[index]).wait_recv()
            face_copy(opposite[index]).wait_recv()

    for index, (dx, dy) in enumerate(DIRECTIONS):
        x = 0 if dx < 0 else n_x - 1
        y = 0 if dy < 0 else n_y - 1
        for half in range(halves):
            base = half * padded_nodes
            if dy == 0:
                codes_ref[pl.ds(base + x * n_y + 1, own_y), :] = recv_code[
                    index, pl.ds(half * own_y, own_y), :
                ]
            elif dx == 0:
                for i in range(own_x):
                    codes_ref[pl.ds(base + (i + 1) * n_y + y, 1), :] = recv_code[
                        index, pl.ds(half * own_y + i, 1), :
                    ]
            else:
                codes_ref[pl.ds(base + x * n_y + y, 1), :] = recv_code[
                    index, pl.ds(half * own_y, 1), :
                ]
        for nodes, run in each_run(index):
            node_ref[nodes, :] = node_ref[nodes, :] + recvs[index][run, :]

    groups = padded_nodes // SUB

    def update(step, carry):
        half = step // groups
        group = step % groups
        base = half * plane + group * (SUB * SUB)
        channels = [
            node_ref[pl.ds(base + c, SUB, stride=SUB), :] for c in range(SUB)
        ]
        code = codes_ref[pl.ds(pl.multiple_of(step * SUB, SUB), SUB), :]
        shifted = code + (code >= 13).astype(jnp.int32)
        normal = [shifted // 9 - 1, shifted // 3 % 3 - 1, shifted % 3 - 1]
        normal = [n.astype(F32) for n in normal]
        length = jnp.sqrt(
            normal[0] * normal[0] + normal[1] * normal[1] + normal[2] * normal[2]
        )
        length = jnp.maximum(length, 1.0)
        normal = [n / length for n in normal]
        masses = [channels[0], channels[4]]
        momenta = [channels[1:4], channels[5:8]]
        gravity = [0.0, 0.0, DT * GRAVITY]
        speeds = [
            [p / jnp.maximum(masses[f], FLOOR) + gravity[r] for r, p in enumerate(momenta[f])]
            for f in range(2)
        ]
        both = jnp.maximum(masses[0] + masses[1], FLOOR)
        center = [
            (momenta[0][r] + momenta[1][r]) / both + gravity[r] for r in range(3)
        ]
        share = jnp.minimum(1.0, jnp.minimum(masses[0], masses[1]) / FLOOR)
        closing = [
            share
            * jnp.maximum(
                sum((speeds[0][r] - center[r]) * normal[r] for r in range(3)), 0.0
            ),
            share
            * jnp.maximum(
                sum((center[r] - speeds[1][r]) * normal[r] for r in range(3)), 0.0
            ),
        ]
        node = group * SUB + lax.broadcasted_iota(jnp.int32, (SUB, LANES), 0)
        x = me_x * own_x + node // n_y
        y = me_y * own_y + node % n_y
        inside = (x >= 1) & (x <= size_x * own_x) & (y >= 1) & (y <= size_y * own_y)
        rows = pl.ds(pl.multiple_of(group * SUB, SUB), SUB)
        for f, sign in ((0, -1.0), (1, 1.0)):
            for r in range(3):
                speed = speeds[f][r] + sign * closing[f] * normal[r]
                planes_ref[half * 6 + 3 * f + r, rows, :] = jnp.where(inside, speed, 0.0)
        return carry

    lax.fori_loop(0, halves * groups, update, 0)
    edge = jnp.zeros((SUB, LANES), F32)
    depth = halves * LANES
    speed_ref[pl.ds(0, SUB), :] = edge
    speed_ref[pl.ds((depth + 1) * SUB, SUB), :] = edge
    for half in range(halves):
        for c in range(6):
            channel = c // 3 * 4 + c % 3
            speed_ref[
                pl.ds((1 + half * LANES) * SUB + channel, LANES, stride=SUB), :
            ] = planes_ref[half * 6 + c].T
        for channel in (3, 7):
            speed_ref[
                pl.ds((1 + half * LANES) * SUB + channel, LANES, stride=SUB), :
            ] = jnp.zeros((LANES, LANES), F32)

    for index in range(8):

        @pl.when(valid[index])
        def _(index=index):
            code_copy(index).wait_send()
            face_copy(index).wait_send()


def gather_kernel(
    shape,
    tile_ref,
    count_ref,
    speed_ref,
    offset_ref,
    deform_ref,
    cell_ref,
    body_ref,
    new_velocity_ref,
    new_affine_ref,
    new_deform_ref,
    new_stress_ref,
    result_ref,
    rows_ref,
):
    n_y, padded_nodes, tiles, unroll = shape
    blocks = cell_ref.shape[0]
    store_rows(rows_ref, blocks, offset_ref, cell_ref)
    coordinates = node_coordinates(n_y, padded_nodes)

    def block_speeds(block):
        tile = tile_ref[block]
        planes = plane_weights(rows_ref, blocks, block, tile, tiles, coordinates)
        start = pl.multiple_of(tile % tiles[1] * (TILE_Z * SUB), SUB)
        speeds = speed_ref[pl.ds(start, SPAN_Z * SUB), :]
        left_high, left_low = split(speeds)
        right_high, right_low = split(jnp.concatenate(planes, 1))
        product = jnp.dot(
            jnp.concatenate([left_high, left_low, left_high], 1),
            jnp.concatenate([right_high, right_high, right_low], 0),
            preferred_element_type=F32,
        )
        sums = [jnp.zeros((SUB, LANES), F32) for _ in range(4)]
        for k in range(SPAN_Z):
            weight = rows_ref[pl.ds((14 + k) * blocks + block, 1), :]
            moment = rows_ref[pl.ds((14 + SPAN_Z + k) * blocks + block, 1), :]
            rows = [product[k * SUB : (k + 1) * SUB, v * LANES : (v + 1) * LANES] for v in range(3)]
            sums[0] = sums[0] + rows[0] * weight
            sums[1] = sums[1] + rows[1] * weight
            sums[2] = sums[2] + rows[2] * weight
            sums[3] = sums[3] + rows[0] * moment
        return sums

    def step(index, carry):
        members = [index * unroll + u for u in range(unroll)]
        results = [block_speeds(block) for block in members]
        for block, sums in zip(members, results):
            for v in range(4):
                start = pl.multiple_of(v * blocks * SUB + block * SUB, SUB)
                result_ref[pl.ds(start, SUB), :] = sums[v]
        return carry

    lax.fori_loop(0, blocks // unroll, step, 0)
    slot = lax.broadcasted_iota(jnp.int32, cell_ref.shape, 0)
    live = slot < count_ref[0, 0]
    even = body_ref[...] % 2 == 0

    def take(v, r):
        fields = [
            result_ref[pl.ds(v * blocks * SUB + 4 * f + r, blocks, stride=SUB), :]
            for f in range(2)
        ]
        return jnp.where(live, jnp.where(even, fields[0], fields[1]), 0.0)

    for r in range(3):
        new_velocity_ref[r] = take(0, r)
    affine = [4.0 * take(1 + c, r) for r in range(3) for c in range(3)]
    deform = [deform_ref[i] for i in range(9)]
    moved = []
    for r in range(3):
        for c in range(3):
            entry = deform[3 * r + c]
            for i in range(3):
                entry = entry + DT * affine[3 * r + i] * deform[3 * i + c]
            moved.append(jnp.where(live, entry, 0.0))
    for i in range(9):
        new_affine_ref[i] = affine[i]
        new_deform_ref[i] = moved[i]
    for i, entry in enumerate(kirchhoff(moved)):
        new_stress_ref[i] = jnp.where(live, entry, 0.0)


def per_device(
    offset,
    particle_mass,
    velocity,
    affine,
    deform,
    particle_cell,
    body_id,
    slot_tile_number,
    block_count,
    normal_code,
):
    blocks, particles = particle_mass.shape
    own_x, own_y, depth = normal_code.shape
    tiles = (own_y // TILE_Y, depth // TILE_Z)
    n_x, n_y = own_x + 2, own_y + 2
    padded_nodes = -(-n_x * n_y // SUB) * SUB
    halves = depth // LANES
    assert particles == LANES and padded_nodes <= LANES and depth % LANES == 0
    unroll = 2 if blocks % 2 == 0 else 1
    vmem = pl.BlockSpec(memory_space=pltpu.VMEM)
    smem = pl.BlockSpec(memory_space=pltpu.SMEM)
    limit = 40 * 1024 * 1024
    grid_shape = jax.ShapeDtypeStruct(((depth + 2) * SUB, LANES), F32)
    work = (n_y, padded_nodes, tiles, unroll)
    node_sums = pl.pallas_call(
        functools.partial(scatter_kernel, work),
        out_shape=grid_shape,
        in_specs=[smem, smem] + [vmem] * 7,
        out_specs=vmem,
        scratch_shapes=[
            pltpu.VMEM((4 * blocks * SUB, LANES), F32),
            pltpu.VMEM((N_ROWS * blocks, LANES), F32),
        ],
        compiler_params=pltpu.CompilerParams(vmem_limit_bytes=limit),
        name="particles_to_nodes",
    )(
        slot_tile_number,
        block_count,
        offset,
        particle_mass,
        velocity,
        affine,
        deform,
        particle_cell,
        body_id,
    )
    faces = [
        pltpu.VMEM((halves * face_nodes(d, n_x, n_y) * SUB, LANES), F32) for d in DIRECTIONS
    ]
    speeds = pl.pallas_call(
        functools.partial(exchange_kernel, (n_x, n_y, padded_nodes, halves)),
        out_shape=grid_shape,
        in_specs=[vmem, vmem],
        out_specs=vmem,
        scratch_shapes=[
            pltpu.VMEM((halves * padded_nodes * SUB, LANES), F32),
            pltpu.VMEM((halves * padded_nodes, LANES), jnp.int32),
            pltpu.VMEM((halves * 6, LANES, LANES), F32),
            pltpu.VMEM((8, halves * own_y, LANES), jnp.int32),
            pltpu.VMEM((8, halves * own_y, LANES), jnp.int32),
        ]
        + faces
        + faces
        + [pltpu.SemaphoreType.DMA((8,))] * 4,
        compiler_params=pltpu.CompilerParams(
            collective_id=0, has_side_effects=True, vmem_limit_bytes=limit
        ),
        name="node_exchange",
    )(node_sums, normal_code)
    shaped = lambda n: jax.ShapeDtypeStruct((n, blocks, LANES), F32)
    return pl.pallas_call(
        functools.partial(gather_kernel, work),
        out_shape=(shaped(3), shaped(9), shaped(9), shaped(6)),
        in_specs=[smem, smem] + [vmem] * 5,
        out_specs=(vmem,) * 4,
        scratch_shapes=[
            pltpu.VMEM((4 * blocks * SUB, LANES), F32),
            pltpu.VMEM((N_ROWS * blocks, LANES), F32),
        ],
        compiler_params=pltpu.CompilerParams(vmem_limit_bytes=limit),
        name="nodes_to_particles",
    )(slot_tile_number, block_count, speeds, offset, deform, particle_cell, body_id)


def solution(mesh):
    particle = P(None, ("gx", "gy"), None)
    flat = P(("gx", "gy"), None)
    placed = (
        particle,
        flat,
        particle,
        particle,
        particle,
        flat,
        flat,
        P(("gx", "gy")),
        P("gx", "gy"),
        P("gx", "gy", None),
    )
    return jax.shard_map(
        per_device,
        mesh=mesh,
        in_specs=placed,
        out_specs=(particle,) * 4,
        check_vma=False,
    )
```

time: 288 us -> 36.1 us (0.13)
  other arithmetic: 138 us -> 0 us
  local copies, waits for them, and re-layouts: 86.5 us -> 6.1 us
  Pallas kernels: 0 us -> 28.1 us
  matrix products: 26 us -> 0 us
  starting transfers between devices: 24.9 us -> 0 us
  waiting for transfers between devices: 6.22 us -> 0 us
    mul x39 -> x0, other arithmetic: 66.7 us -> none  [the longest x6 16 us: build_weights(): weight_x * shared_yz]
    scatter-add x3 -> x0, other arithmetic: 56 us -> none  [the longest x1 55.9 us: per_device(): node_grid = node_grid.at[:, flat_index].add(patches)]
    gather x2 -> x0, local copies, waits for them, and re-layouts: 39 us -> none  [per_device(): block_speeds = flat_speeds[:, flat_index]]
    pallas_call x0 -> x3, Pallas kernels: none -> 28.1 us  [the longest x1 17.5 us: per_device(): pl.pallas_call(functools.partial(exchange_kernel, (n_x, n_y, padded_nodes...]
    dot_general x6 -> x0, matrix products: 26 us -> none  [the longest x3 15.9 us: gather_work(): jnp.einsum('glpq,cgq->lcgp', kernel, speed_rows, precision=lax.Precision....]
    ppermute x8 -> x0, starting transfers between devices: 24.9 us -> none  [the longest x4 11 us: from_behind(): return lax.ppermute(block, axis, route)]
    slice x6 -> x0, local copies, waits for them, and re-layouts: 18 us -> none  [the longest x2 17.7 us: per_device(): node_grid[:, :grid_cells]]
    concatenate x1 -> x0, local copies, waits for them, and re-layouts: 9.68 us -> none  [per_device(): jnp.concatenate([speeds.reshape(6, -1), jnp.zeros((6, 1), jnp.float32)], 1)]
  transfers between devices with their start and end apart: 8 -> 0, of which waited for: 5 -> 0; matrix products, arithmetic and copies ran while one was open for 2% -> 0% of each run, Pallas kernels for 0% -> 0%
where the time goes in v1:
time: 36.1 us; the launch traced here: 35.5 us
  Pallas kernels  28.1 us (78%)
  local copies, waits for them, and re-layouts  6.1 us (17%)
  between operations  1.32 us (4%)
    pallas_call x1, Pallas kernels, per_device(): pl.pallas_call(functools.partial(exchange_kernel, (n_x, n_y, padded_nodes...  17.5 us
    unnamed x18, local copies, waits for them, and re-layouts  6.1 us
    pallas_call x1, Pallas kernels, per_device(): pl.pallas_call(functools.partial(gather_kernel, work), out_shape=(shaped(...  5.47 us
    pallas_call x1, Pallas kernels, per_device(): pl.pallas_call(functools.partial(scatter_kernel, work), out_shape=grid_sh...  5.12 us

profile of v1, /device:TPU:13, one launch (start us, length us, event | category | flops | bytes accessed | tf_op | source)
XLA Modules:
  0.0 35.5 jit_solution(10804845874090527918)
XLA Ops:
  1.3 0.0 copy-start
  1.3 0.9 %copy-done = f32[9,24,128]{2,1,0:T(8,128)S(1)} copy-done((f32[9,24,128]{2,1,0:T(8,128)S(1)}, f32[9,24,128]{2,1,0:T(8,128)}, u32[]{:S(2)}) %copy-start) | copy-done | bytes 110616
  2.2 0.0 copy-start.1
  2.2 0.8 %copy-done.1 = f32[3,24,128]{2,1,0:T(8,128)S(1)} copy-done((f32[3,24,128]{2,1,0:T(8,128)S(1)}, f32[3,24,128]{2,1,0:T(8,128)}, u32[]{:S(2)}) %copy-start.1) | copy-done | bytes 36888
  2.9 0.0 copy-start.2
  2.9 0.9 %copy-done.2 = f32[9,24,128]{2,1,0:T(8,128)S(1)} copy-done((f32[9,24,128]{2,1,0:T(8,128)S(1)}, f32[9,24,128]{2,1,0:T(8,128)}, u32[]{:S(2)}) %copy-start.2) | copy-done | bytes 110616
  3.8 0.0 copy-start.4
  3.8 0.7 %copy-done.4 = s32[24,128]{1,0:T(8,128)S(1)} copy-done((s32[24,128]{1,0:T(8,128)S(1)}, s32[24,128]{1,0:T(8,128)}, u32[]{:S(2)}) %copy-start.4) | copy-done | bytes 12312
  4.6 0.0 copy-start.5
  4.6 0.7 %copy-done.5 = s32[24,128]{1,0:T(8,128)S(1)} copy-done((s32[24,128]{1,0:T(8,128)S(1)}, s32[24,128]{1,0:T(8,128)}, u32[]{:S(2)}) %copy-start.5) | copy-done | bytes 12312
  5.3 0.0 copy-start.6
  5.3 0.8 %copy-done.6 = f32[3,24,128]{2,1,0:T(8,128)S(1)} copy-done((f32[3,24,128]{2,1,0:T(8,128)S(1)}, f32[3,24,128]{2,1,0:T(8,128)}, u32[]{:S(2)}) %copy-start.6) | copy-done | bytes 36888
  6.0 0.0 copy-start.7
  6.0 0.7 %copy-done.7 = f32[24,128]{1,0:T(8,128)S(1)} copy-done((f32[24,128]{1,0:T(8,128)S(1)}, f32[24,128]{1,0:T(8,128)}, u32[]{:S(2)}) %copy-start.7) | copy-done | bytes 12312
  6.7 0.0 copy-start.8
  6.7 0.7 %copy-done.8 = s32[24]{0:T(128)S(1)} copy-done((s32[24]{0:T(128)S(1)}, s32[24]{0:T(128)}, u32[]{:S(2)}) %copy-start.8) | copy-done | bytes 120
  7.4 0.0 copy-start.3
  7.4 5.1 %particles_to_nodes.1.grid_ref = f32[2064,128]{1,0:T(8,128)S(1)} custom-call(s32[24]{0:T(128)S(1)} %copy-done.8, s32[1,1]{1,0:T(1,128)S(6)} %copy.14.count_ref, f32[3,24,128]{2,1,0:T(8,128)S(1)} %copy-done.1, f32[24,128]{1,0:T(8,128)S(1)} %copy-done.7, f32[3,24,128]{2,1,0:T(8,128)S(1)} %copy-done.6, f32[9,24,128]{2,1,0:T(8,128)S(1)} %copy-done.2, ...), custom_call_target="tpu_custom_call" | custom-call | tf_op jit(solution)/shard_map/particles_to_nodes/pallas_call | solution.py:542
  12.5 0.0 copy-done.3
  12.5 17.5 %node_exchange.1.speed_ref = f32[2064,128]{1,0:T(8,128)S(1)} custom-call(f32[2064,128]{1,0:T(8,128)S(1)} %particles_to_nodes.1.grid_ref, s32[8,8,256]{2,1,0:T(8,128)S(1)} %copy-done.3), custom_call_target="tpu_custom_call" | custom-call | tf_op jit(solution)/shard_map/node_exchange/pallas_call | solution.py:567
  30.0 5.5 %nodes_to_particles.1 = (f32[3,24,128]{2,1,0:T(8,128)}, f32[9,24,128]{2,1,0:T(8,128)}, f32[9,24,128]{2,1,0:T(8,128)}, f32[6,24,128]{2,1,0:T(8,128)}) custom-call(s32[24]{0:T(128)S(1)} %copy-done.8, s32[1,1]{1,0:T(1,128)S(6)} %copy.14.count_ref, f32[2064,128]{1,0:T(8,128)S(1)} %node_exchange.1.speed_ref, f32[3,24,128]{2,1,0:T(8,128)S(1)} %copy-done.1, ...), custom_call_target="tpu_custom_call" | custom-call | tf_op jit(solution)/shard_map/nodes_to_particles/pallas_call | solution.py:588
Async XLA Ops:
  1.3 0.9 %copy-start = (f32[9,24,128]{2,1,0:T(8,128)S(1)}, f32[9,24,128]{2,1,0:T(8,128)}, u32[]{:S(2)}) copy-start(f32[9,24,128]{2,1,0:T(8,128)} %deform_ref.3) | copy-start | bytes 331780
  2.2 0.8 %copy-start.1 = (f32[3,24,128]{2,1,0:T(8,128)S(1)}, f32[3,24,128]{2,1,0:T(8,128)}, u32[]{:S(2)}) copy-start(f32[3,24,128]{2,1,0:T(8,128)} %offset_ref.3) | copy-start | bytes 110596
  2.9 0.9 %copy-start.2 = (f32[9,24,128]{2,1,0:T(8,128)S(1)}, f32[9,24,128]{2,1,0:T(8,128)}, u32[]{:S(2)}) copy-start(f32[9,24,128]{2,1,0:T(8,128)} %affine_ref.1) | copy-start | bytes 331780
  3.8 0.7 %copy-start.4 = (s32[24,128]{1,0:T(8,128)S(1)}, s32[24,128]{1,0:T(8,128)}, u32[]{:S(2)}) copy-start(s32[24,128]{1,0:T(8,128)} %cell_ref.3) | copy-start | bytes 36868
  4.6 0.7 %copy-start.5 = (s32[24,128]{1,0:T(8,128)S(1)}, s32[24,128]{1,0:T(8,128)}, u32[]{:S(2)}) copy-start(s32[24,128]{1,0:T(8,128)} %body_ref.3) | copy-start | bytes 36868
  5.3 0.8 %copy-start.6 = (f32[3,24,128]{2,1,0:T(8,128)S(1)}, f32[3,24,128]{2,1,0:T(8,128)}, u32[]{:S(2)}) copy-start(f32[3,24,128]{2,1,0:T(8,128)} %velocity_ref.1) | copy-start | bytes 110596
  6.0 0.7 %copy-start.7 = (f32[24,128]{1,0:T(8,128)S(1)}, f32[24,128]{1,0:T(8,128)}, u32[]{:S(2)}) copy-start(f32[24,128]{1,0:T(8,128)} %mass_ref.1) | copy-start | bytes 36868
  6.7 0.7 %copy-start.8 = (s32[24]{0:T(128)S(1)}, s32[24]{0:T(128)}, u32[]{:S(2)}) copy-start(s32[24]{0:T(128)} %tile_ref.3) | copy-start | bytes 292
  7.4 5.1 %copy-start.3 = (s32[8,8,256]{2,1,0:T(8,128)S(1)}, s32[8,8,256]{2,1,0:T(8,128)}, u32[]{:S(2)}) copy-start(s32[8,8,256]{2,1,0:T(8,128)} %code_ref.1) | copy-start | bytes 196612

commit v2 on v1

--- a/solution.py
+++ b/solution.py
@@ -19,6 +19,7 @@
 MESH = pl.DeviceIdType.MESH
 F32 = jnp.float32
 BF16 = jnp.bfloat16
+SIDES = [(-1, 0), (1, 0), (0, -1), (0, 1)]
 DIRECTIONS = [(-1, 0), (1, 0), (0, -1), (0, 1), (-1, -1), (-1, 1), (1, -1), (1, 1)]
 
 
@@ -86,9 +87,9 @@
 N_ROWS = 14 + 2 * SPAN_Z
 
 
-def node_coordinates(n_y, padded_nodes):
+def node_coordinates(n_x, padded_nodes):
     node = lax.broadcasted_iota(jnp.int32, (padded_nodes, LANES), 0)
-    return (node // n_y).astype(F32), (node % n_y).astype(F32)
+    return (node % n_x).astype(F32), (node // n_x).astype(F32)
 
 
 def plane_weights(rows_ref, blocks, block, tile, tiles, coordinates):
@@ -115,23 +116,119 @@
     return [jnp.concatenate([p, pad], 0) for p in out]
 
 
-def scatter_kernel(
+def face_runs(kind, side, n_x, n_y):
+    if kind == "x":
+        first = 0 if side < 0 else n_x - 2
+        return [(y * n_x + first, 2) for y in range(n_y)]
+    layers = (0, 1) if side < 0 else (n_y - 2, n_y - 1)
+    if kind == "inner":
+        return [(y * n_x + 2, n_x - 4) for y in layers]
+    return [(y * n_x + first, 2) for y in layers for first in (0, n_x - 2)]
+
+
+FACES = [("x", -1), ("x", 1), ("inner", -1), ("inner", 1), ("outer", -1), ("outer", 1)]
+
+
+def nodes_kernel(
     shape,
     tile_ref,
     count_ref,
-    offset_ref,
-    mass_ref,
-    velocity_ref,
-    affine_ref,
-    deform_ref,
-    cell_ref,
-    body_ref,
-    grid_ref,
-    source_ref,
-    rows_ref,
+    offset_hbm,
+    mass_hbm,
+    velocity_hbm,
+    affine_hbm,
+    deform_hbm,
+    cell_hbm,
+    body_hbm,
+    code_hbm,
+    speed_ref,
+    *scratch,
 ):
-    n_y, padded_nodes, tiles, unroll = shape
+    n_x, n_y, padded_nodes, halves, tiles, unroll = shape
+    inputs = scratch[:8]
+    offset_ref, mass_ref, velocity_ref, affine_ref, deform_ref = inputs[:5]
+    cell_ref, body_ref, code_ref = inputs[5:]
+    (
+        source_ref,
+        rows_ref,
+        chain_ref,
+        grid_ref,
+        table_ref,
+        links,
+        node_ref,
+        codes_ref,
+        planes_ref,
+        send_code,
+        recv_code,
+    ) = scratch[8:19]
+    sends = scratch[19:25]
+    recvs = scratch[25:31]
+    send_sem, recv_sem, code_send_sem, code_recv_sem, in_sem, table_sem = scratch[31:]
     blocks = mass_ref.shape[0]
+    size_x, size_y = lax.axis_size("gx"), lax.axis_size("gy")
+    me_x, me_y = lax.axis_index("gx"), lax.axis_index("gy")
+    own_x, own_y = n_x - 2, n_y - 2
+
+    hbm = (
+        offset_hbm,
+        mass_hbm,
+        velocity_hbm,
+        affine_hbm,
+        deform_hbm,
+        cell_hbm,
+        body_hbm,
+        code_hbm,
+    )
+    loads = [
+        pltpu.make_async_copy(source, target, in_sem.at[i])
+        for i, (source, target) in enumerate(zip(hbm, inputs))
+    ]
+    for load in loads:
+        load.start()
+
+    valid = []
+    for dx, dy in DIRECTIONS:
+        ok = None
+        for d, me, size in ((dx, me_x, size_x), (dy, me_y, size_y)):
+            if d == 0:
+                continue
+            one = me > 0 if d < 0 else me < size - 1
+            ok = one if ok is None else jnp.logical_and(ok, one)
+        valid.append(ok)
+    barrier = pltpu.get_barrier_semaphore()
+
+    def target(index):
+        dx, dy = DIRECTIONS[index]
+        return {"gx": me_x + dx, "gy": me_y + dy}
+
+    for index in range(8):
+
+        @pl.when(valid[index])
+        def _(index=index):
+            pl.semaphore_signal(
+                barrier, inc=1, device_id=target(index), device_id_type=MESH
+            )
+
+    opposite = [DIRECTIONS.index((-dx, -dy)) for dx, dy in DIRECTIONS]
+    plane = padded_nodes * SUB
+
+    lane = lax.broadcasted_iota(jnp.int32, (SUB, LANES), 1)
+    heights = [tile_ref[s] % tiles[1] for s in range(blocks)]
+    height = jnp.full((SUB, LANES), -1, jnp.int32)
+    for s in range(blocks):
+        height = jnp.where(lane == s, heights[s], height)
+    before = jnp.zeros((SUB, LANES), jnp.int32)
+    last = jnp.zeros((SUB, LANES), jnp.int32)
+    for s in range(blocks):
+        before = jnp.where((height == heights[s]) & (lane > s), s + 1, before)
+        last = jnp.where(lane == heights[s], s + 1, last)
+    sublane = lax.broadcasted_iota(jnp.int32, (SUB, LANES), 0)
+    table_ref[...] = jnp.where(sublane == 0, before, last)
+    table_copy = pltpu.make_async_copy(table_ref, links, table_sem)
+    table_copy.start()
+
+    for load in loads[:7]:
+        load.wait()
     slot = lax.broadcasted_iota(jnp.int32, mass_ref.shape, 0)
     mass = jnp.where(slot < count_ref[0, 0], mass_ref[...], 0.0)
     even = body_ref[...] % 2 == 0
@@ -152,8 +249,10 @@
             for r in range(3):
                 put(1 + c, 4 * field + 1 + r, masses[field] * force[3 * r + c])
     store_rows(rows_ref, blocks, offset_ref, cell_ref)
-    grid_ref[...] = jnp.zeros_like(grid_ref)
-    coordinates = node_coordinates(n_y, padded_nodes)
+    coordinates = node_coordinates(n_x, padded_nodes)
+    span = SPAN_Z * SUB
+    chain_ref[0] = jnp.zeros((span, LANES), F32)
+    table_copy.wait()
 
     def block_sums(block):
         tile = tile_ref[block]
@@ -181,69 +280,18 @@
             (((1,), (1,)), ((), ())),
             preferred_element_type=F32,
         )
-        n = SPAN_Z * SUB
-        return product[:n, :LANES] + (product[:n, LANES:] + product[n:, :LANES])
+        return product[:span, :LANES] + (product[:span, LANES:] + product[span:, :LANES])
 
     def step(index, carry):
         members = [index * unroll + u for u in range(unroll)]
         sums = [block_sums(block) for block in members]
         for block, patch in zip(members, sums):
-            start = pl.multiple_of(tile_ref[block] % tiles[1] * (TILE_Z * SUB), SUB)
-            window = pl.ds(start, SPAN_Z * SUB)
-            grid_ref[window, :] = grid_ref[window, :] + patch
+            chain_ref[block + 1] = chain_ref[links[0, block]] + patch
         return carry
 
     lax.fori_loop(0, blocks // unroll, step, 0)
 
-
-def face_runs(direction, n_x, n_y):
-    dx, dy = direction
-    xs = {-1: (0, 2), 0: (0, n_x), 1: (n_x - 2, 2)}[dx]
-    ys = {-1: (0, 2), 0: (0, n_y), 1: (n_y - 2, 2)}[dy]
-    if dy == 0:
-        return [(xs[0] * n_y, xs[1] * n_y)]
-    return [((xs[0] + i) * n_y + ys[0], ys[1]) for i in range(xs[1])]
-
-
-def face_nodes(direction, n_x, n_y):
-    return sum(count for _, count in face_runs(direction, n_x, n_y))
-
-
-def exchange_kernel(shape, grid_ref, code_ref, speed_ref, *scratch):
-    n_x, n_y, padded_nodes, halves = shape
-    node_ref, codes_ref, planes_ref, send_code, recv_code = scratch[:5]
-    sends = scratch[5:13]
-    recvs = scratch[13:21]
-    send_sem, recv_sem, code_send_sem, code_recv_sem = scratch[21:]
-    size_x, size_y = lax.axis_size("gx"), lax.axis_size("gy")
-    me_x, me_y = lax.axis_index("gx"), lax.axis_index("gy")
-    own_x, own_y = n_x - 2, n_y - 2
-    valid = []
-    for dx, dy in DIRECTIONS:
-        ok = None
-        for d, me, size in ((dx, me_x, size_x), (dy, me_y, size_y)):
-            if d == 0:
-                continue
-            one = me > 0 if d < 0 else me < size - 1
-            ok = one if ok is None else jnp.logical_and(ok, one)
-        valid.append(ok)
-    barrier = pltpu.get_barrier_semaphore()
-
-    def target(index):
-        dx, dy = DIRECTIONS[index]
-        return {"gx": me_x + dx, "gy": me_y + dy}
-
-    for index in range(8):
-
-        @pl.when(valid[index])
-        def _(index=index):
-            pl.semaphore_signal(
-                barrier, inc=1, device_id=target(index), device_id_type=MESH
-            )
-
-    opposite = [DIRECTIONS.index((-dx, -dy)) for dx, dy in DIRECTIONS]
-    plane = padded_nodes * SUB
-
+    loads[7].wait()
     for half in range(halves):
         lanes = pl.ds(half * LANES, LANES)
         rows = pl.ds(half * own_y, own_y)
@@ -272,15 +320,43 @@
             device_id_type=MESH,
         )
 
-    def face_copy(index):
+    def face_copy(face):
         return pltpu.make_async_remote_copy(
-            src_ref=sends[index],
-            dst_ref=recvs[opposite[index]],
-            send_sem=send_sem.at[index],
-            recv_sem=recv_sem.at[opposite[index]],
-            device_id=target(index),
+            src_ref=sends[face],
+            dst_ref=recvs[face ^ 1],
+            send_sem=send_sem.at[face],
+            recv_sem=recv_sem.at[face ^ 1],
+            device_id=target(min(face, 2 + face % 2)),
             device_id_type=MESH,
         )
+
+    def face_valid(face):
+        return valid[min(face, 2 + face % 2)]
+
+    arrivals = sum(ok.astype(jnp.int32) for ok in valid)
+    pl.semaphore_wait(barrier, arrivals)
+    for index in range(8):
+
+        @pl.when(valid[index])
+        def _(index=index):
+            code_copy(index).start()
+
+        @pl.when(jnp.logical_not(valid[index]))
+        def _(index=index):
+            recv_code[index] = jnp.zeros(recv_code.shape[1:], jnp.int32)
+
+    body_rows = TILE_Z * SUB
+    over = span - body_rows
+
+    def assemble(j, carry):
+        patch = chain_ref[links[1, j]]
+        rows = pl.multiple_of(j * body_rows, SUB)
+        grid_ref[pl.ds(rows, over), :] = patch[:over] + carry
+        grid_ref[pl.ds(rows + over, body_rows - over), :] = patch[over:body_rows]
+        return patch[body_rows:]
+
+    tail = lax.fori_loop(0, tiles[1], assemble, jnp.zeros((over, LANES), F32), unroll=4)
+    grid_ref[pl.ds(tiles[1] * body_rows, over), :] = tail
 
     for half in range(halves):
         for c in range(SUB):
@@ -289,90 +365,93 @@
                 :padded_nodes
             ]
 
-    def each_run(index):
+    def each_run(face):
         offset = 0
         for half in range(halves):
-            for first, count in face_runs(DIRECTIONS[index], n_x, n_y):
+            for first, count in face_runs(*FACES[face], n_x, n_y):
                 yield (
                     pl.ds(half * plane + first * SUB, count * SUB),
                     pl.ds(offset, count * SUB),
                 )
                 offset += count * SUB
 
-    for index in range(8):
-        for nodes, run in each_run(index):
-            sends[index][run, :] = node_ref[nodes, :]
-
-    arrivals = sum(ok.astype(jnp.int32) for ok in valid)
-    pl.semaphore_wait(barrier, arrivals)
-    for index in [2, 3, 4, 5, 6, 7, 0, 1]:
-
-        @pl.when(valid[index])
-        def _(index=index):
-            code_copy(index).start()
-            face_copy(index).start()
-
-        @pl.when(jnp.logical_not(valid[index]))
-        def _(index=index):
-            recv_code[index] = jnp.zeros(recv_code.shape[1:], jnp.int32)
-            recvs[index][...] = jnp.zeros_like(recvs[index])
+    def send_face(face):
+        for nodes, run in each_run(face):
+            sends[face][run, :] = node_ref[nodes, :]
+
+        @pl.when(face_valid(face))
+        def _():
+            face_copy(face).start()
+
+        @pl.when(jnp.logical_not(face_valid(face)))
+        def _():
+            recvs[face][...] = jnp.zeros_like(recvs[face])
+
+    def take_face(face):
+        @pl.when(face_valid(face))
+        def _():
+            face_copy(face ^ 1).wait_recv()
+
+        for nodes, run in each_run(face):
+            node_ref[nodes, :] = node_ref[nodes, :] + recvs[face][run, :]
+
+    for face in (0, 1, 2, 3):
+        send_face(face)
 
     codes_ref[...] = jnp.zeros_like(codes_ref)
     for half in range(halves):
         lanes = pl.ds(half * LANES, LANES)
         for x in range(own_x):
-            codes_ref[pl.ds(half * padded_nodes + (x + 1) * n_y + 1, own_y), :] = code_ref[
-                x, :, lanes
-            ]
+            codes_ref[
+                pl.ds(half * padded_nodes + n_x + x + 1, own_y, stride=n_x), :
+            ] = code_ref[x, :, lanes]
     planes_ref[:, pl.ds(padded_nodes, LANES - padded_nodes), :] = jnp.zeros(
         (planes_ref.shape[0], LANES - padded_nodes, LANES), F32
     )
-
-    for index in [0, 1, 4, 5, 6, 7, 2, 3]:
+    for index, (dx, dy) in enumerate(DIRECTIONS):
 
         @pl.when(valid[index])
         def _(index=index):
             code_copy(opposite[index]).wait_recv()
-            face_copy(opposite[index]).wait_recv()
-
-    for index, (dx, dy) in enumerate(DIRECTIONS):
+
         x = 0 if dx < 0 else n_x - 1
         y = 0 if dy < 0 else n_y - 1
         for half in range(halves):
             base = half * padded_nodes
+            rows = pl.ds(half * own_y, own_y)
             if dy == 0:
-                codes_ref[pl.ds(base + x * n_y + 1, own_y), :] = recv_code[
-                    index, pl.ds(half * own_y, own_y), :
+                codes_ref[pl.ds(base + n_x + x, own_y, stride=n_x), :] = recv_code[
+                    index, rows, :
                 ]
             elif dx == 0:
-                for i in range(own_x):
-                    codes_ref[pl.ds(base + (i + 1) * n_y + y, 1), :] = recv_code[
-                        index, pl.ds(half * own_y + i, 1), :
-                    ]
+                codes_ref[pl.ds(base + y * n_x + 1, own_x), :] = recv_code[
+                    index, pl.ds(half * own_y, own_x), :
+                ]
             else:
-                codes_ref[pl.ds(base + x * n_y + y, 1), :] = recv_code[
+                codes_ref[pl.ds(base + y * n_x + x, 1), :] = recv_code[
                     index, pl.ds(half * own_y, 1), :
                 ]
-        for nodes, run in each_run(index):
-            node_ref[nodes, :] = node_ref[nodes, :] + recvs[index][run, :]
+
+    take_face(0)
+    take_face(1)
+    send_face(4)
+    send_face(5)
 
     groups = padded_nodes // SUB
 
-    def update(step, carry):
-        half = step // groups
-        group = step % groups
+    def update(half, group):
         base = half * plane + group * (SUB * SUB)
         channels = [
             node_ref[pl.ds(base + c, SUB, stride=SUB), :] for c in range(SUB)
         ]
-        code = codes_ref[pl.ds(pl.multiple_of(step * SUB, SUB), SUB), :]
+        row = half * padded_nodes + group * SUB
+        code = codes_ref[pl.ds(pl.multiple_of(row, SUB), SUB), :]
         shifted = code + (code >= 13).astype(jnp.int32)
         normal = [shifted // 9 - 1, shifted // 3 % 3 - 1, shifted % 3 - 1]
         normal = [n.astype(F32) for n in normal]
         length = jnp.sqrt(
             normal[0] * normal[0] + normal[1] * normal[1] + normal[2] * normal[2]
         )
-        length = jnp.maximum(length, 1.0)
         normal = [n / length for n in normal]
         masses = [channels[0], channels[4]]
         momenta = [channels[1:4], channels[5:8]]
@@ -397,17 +476,29 @@
             ),
         ]
         node = group * SUB + lax.broadcasted_iota(jnp.int32, (SUB, LANES), 0)
-        x = me_x * own_x + node // n_y
-        y = me_y * own_y + node % n_y
+        x = me_x * own_x + node % n_x
+        y = me_y * own_y + node // n_x
         inside = (x >= 1) & (x <= size_x * own_x) & (y >= 1) & (y <= size_y * own_y)
         rows = pl.ds(pl.multiple_of(group * SUB, SUB), SUB)
         for f, sign in ((0, -1.0), (1, 1.0)):
             for r in range(3):
                 speed = speeds[f][r] + sign * closing[f] * normal[r]
                 planes_ref[half * 6 + 3 * f + r, rows, :] = jnp.where(inside, speed, 0.0)
-        return carry
-
-    lax.fori_loop(0, halves * groups, update, 0)
+
+    def update_groups(first, count):
+        def body(step, carry):
+            update(step // count, first + step % count)
+            return carry
+
+        lax.fori_loop(0, halves * count, body, 0)
+
+    early = -(-2 * n_x // SUB)
+    late = (n_y - 2) * n_x // SUB
+    update_groups(early, late - early)
+    for face in (2, 3, 4, 5):
+        take_face(face)
+    update_groups(0, early)
+    update_groups(late, groups - late)
     edge = jnp.zeros((SUB, LANES), F32)
     depth = halves * LANES
     speed_ref[pl.ds(0, SUB), :] = edge
@@ -428,7 +519,12 @@
         @pl.when(valid[index])
         def _(index=index):
             code_copy(index).wait_send()
-            face_copy(index).wait_send()
+
+    for face in range(6):
+
+        @pl.when(face_valid(face))
+        def _(face=face):
+            face_copy(face).wait_send()
 
 
 def gather_kernel(
@@ -447,10 +543,10 @@
     result_ref,
     rows_ref,
 ):
-    n_y, padded_nodes, tiles, unroll = shape
+    n_x, padded_nodes, tiles, unroll = shape
     blocks = cell_ref.shape[0]
     store_rows(rows_ref, blocks, offset_ref, cell_ref)
-    coordinates = node_coordinates(n_y, padded_nodes)
+    coordinates = node_coordinates(n_x, padded_nodes)
 
     def block_speeds(block):
         tile = tile_ref[block]
@@ -534,42 +630,36 @@
     halves = depth // LANES
     assert particles == LANES and padded_nodes <= LANES and depth % LANES == 0
     unroll = 2 if blocks % 2 == 0 else 1
+    assert own_x == own_y and max(blocks, tiles[1]) <= LANES
     vmem = pl.BlockSpec(memory_space=pltpu.VMEM)
     smem = pl.BlockSpec(memory_space=pltpu.SMEM)
     limit = 40 * 1024 * 1024
     grid_shape = jax.ShapeDtypeStruct(((depth + 2) * SUB, LANES), F32)
-    work = (n_y, padded_nodes, tiles, unroll)
-    node_sums = pl.pallas_call(
-        functools.partial(scatter_kernel, work),
+    work = (n_x, padded_nodes, tiles, unroll)
+    operands = (offset, particle_mass, velocity, affine, deform, particle_cell, body_id)
+    operands = operands + (normal_code,)
+    faces = [
+        pltpu.VMEM(
+            (halves * SUB * sum(count for _, count in face_runs(*face, n_x, n_y)), LANES), F32
+        )
+        for face in FACES
+    ]
+    dma = pltpu.SemaphoreType.DMA
+    speeds = pl.pallas_call(
+        functools.partial(
+            nodes_kernel, (n_x, n_y, padded_nodes, halves, tiles, unroll)
+        ),
         out_shape=grid_shape,
-        in_specs=[smem, smem] + [vmem] * 7,
+        in_specs=[smem, smem] + [pl.BlockSpec(memory_space=pltpu.HBM)] * 8,
         out_specs=vmem,
-        scratch_shapes=[
+        scratch_shapes=[pltpu.VMEM(a.shape, a.dtype) for a in operands]
+        + [
             pltpu.VMEM((4 * blocks * SUB, LANES), F32),
             pltpu.VMEM((N_ROWS * blocks, LANES), F32),
-        ],
-        compiler_params=pltpu.CompilerParams(vmem_limit_bytes=limit),
-        name="particles_to_nodes",
-    )(
-        slot_tile_number,
-        block_count,
-        offset,
-        particle_mass,
-        velocity,
-        affine,
-        deform,
-        particle_cell,
-        body_id,
-    )
-    faces = [
-        pltpu.VMEM((halves * face_nodes(d, n_x, n_y) * SUB, LANES), F32) for d in DIRECTIONS
-    ]
-    speeds = pl.pallas_call(
-        functools.partial(exchange_kernel, (n_x, n_y, padded_nodes, halves)),
-        out_shape=grid_shape,
-        in_specs=[vmem, vmem],
-        out_specs=vmem,
-        scratch_shapes=[
+            pltpu.VMEM((blocks + 1, SPAN_Z * SUB, LANES), F32),
+            pltpu.VMEM(grid_shape.shape, F32),
+            pltpu.VMEM((SUB, LANES), jnp.int32),
+            pltpu.SMEM((SUB, LANES), jnp.int32),
             pltpu.VMEM((halves * padded_nodes * SUB, LANES), F32),
             pltpu.VMEM((halves * padded_nodes, LANES), jnp.int32),
             pltpu.VMEM((halves * 6, LANES, LANES), F32),
@@ -578,12 +668,12 @@
         ]
         + faces
         + faces
-        + [pltpu.SemaphoreType.DMA((8,))] * 4,
+        + [dma((6,)), dma((6,)), dma((8,)), dma((8,)), dma((8,)), dma(())],
         compiler_params=pltpu.CompilerParams(
             collective_id=0, has_side_effects=True, vmem_limit_bytes=limit
         ),
-        name="node_exchange",
-    )(node_sums, normal_code)
+        name="particles_to_node_speeds",
+    )(slot_tile_number, block_count, *operands)
     shaped = lambda n: jax.ShapeDtypeStruct((n, blocks, LANES), F32)
     return pl.pallas_call(
         functools.partial(gather_kernel, work),

time: 36.1 us -> 32.1 us (0.89)
  Pallas kernels: 28.1 us -> 23.3 us
  local copies, waits for them, and re-layouts: 6.1 us -> 6.93 us
    pallas_call x2 -> x1, Pallas kernels: 22.6 us -> 17.8 us  [per_device(): pl.pallas_call(functools.partial(nodes_kernel, (n_x, n_y, padded_nodes, h...]
    unnamed x18, local copies, waits for them, and re-layouts: 6.1 us -> 6.93 us
where the time goes in v2:
time: 32.1 us; the launch traced here: 31.6 us
  Pallas kernels  23.3 us (73%)
  local copies, waits for them, and re-layouts  6.93 us (22%)
  between operations  1.31 us (4%)
    pallas_call x1, Pallas kernels, per_device(): pl.pallas_call(functools.partial(nodes_kernel, (n_x, n_y, padded_nodes, h...  17.8 us
    unnamed x18, local copies, waits for them, and re-layouts  6.93 us
    pallas_call x1, Pallas kernels, per_device(): pl.pallas_call(functools.partial(gather_kernel, work), out_shape=(shaped(...  5.49 us

profile of v2, /device:TPU:13, one launch (start us, length us, event | category | flops | bytes accessed | tf_op | source)
XLA Modules:
  0.0 31.6 jit_solution(8367303228642418791)
XLA Ops:
  1.3 0.0 copy-start
  1.3 0.9 %copy-done = f32[9,24,128]{2,1,0:T(8,128)S(1)} copy-done((f32[9,24,128]{2,1,0:T(8,128)S(1)}, f32[9,24,128]{2,1,0:T(8,128)}, u32[]{:S(2)}) %copy-start) | copy-done | bytes 110616
  2.2 0.0 copy-start.1
  2.2 0.8 %copy-done.1 = f32[3,24,128]{2,1,0:T(8,128)S(1)} copy-done((f32[3,24,128]{2,1,0:T(8,128)S(1)}, f32[3,24,128]{2,1,0:T(8,128)}, u32[]{:S(2)}) %copy-start.1) | copy-done | bytes 36888
  2.9 0.0 copy-start.2
  2.9 0.9 %copy-done.2 = f32[9,24,128]{2,1,0:T(8,128)S(1)} copy-done((f32[9,24,128]{2,1,0:T(8,128)S(1)}, f32[9,24,128]{2,1,0:T(8,128)}, u32[]{:S(2)}) %copy-start.2) | copy-done | bytes 110616
  3.8 0.0 copy-start.3
  3.8 0.8 %copy-done.3 = s32[8,8,256]{2,1,0:T(8,128)S(1)} copy-done((s32[8,8,256]{2,1,0:T(8,128)S(1)}, s32[8,8,256]{2,1,0:T(8,128)}, u32[]{:S(2)}) %copy-start.3) | copy-done | bytes 65560
  4.7 0.0 copy-start.4
  4.7 0.7 %copy-done.4 = s32[24,128]{1,0:T(8,128)S(1)} copy-done((s32[24,128]{1,0:T(8,128)S(1)}, s32[24,128]{1,0:T(8,128)}, u32[]{:S(2)}) %copy-start.4) | copy-done | bytes 12312
  5.4 0.0 copy-start.5
  5.4 0.7 %copy-done.5 = s32[24,128]{1,0:T(8,128)S(1)} copy-done((s32[24,128]{1,0:T(8,128)S(1)}, s32[24,128]{1,0:T(8,128)}, u32[]{:S(2)}) %copy-start.5) | copy-done | bytes 12312
  6.1 0.0 copy-start.6
  6.1 0.8 %copy-done.6 = f32[3,24,128]{2,1,0:T(8,128)S(1)} copy-done((f32[3,24,128]{2,1,0:T(8,128)S(1)}, f32[3,24,128]{2,1,0:T(8,128)}, u32[]{:S(2)}) %copy-start.6) | copy-done | bytes 36888
  6.9 0.0 copy-start.7
  6.9 0.7 %copy-done.7 = f32[24,128]{1,0:T(8,128)S(1)} copy-done((f32[24,128]{1,0:T(8,128)S(1)}, f32[24,128]{1,0:T(8,128)}, u32[]{:S(2)}) %copy-start.7) | copy-done | bytes 12312
  7.6 0.0 copy-start.8
  7.6 0.7 %copy-done.8 = s32[24]{0:T(128)S(1)} copy-done((s32[24]{0:T(128)S(1)}, s32[24]{0:T(128)}, u32[]{:S(2)}) %copy-start.8) | copy-done | bytes 120
  8.2 17.8 %particles_to_node_speeds.1.speed_ref = f32[2064,128]{1,0:T(8,128)S(1)} custom-call(s32[24]{0:T(128)S(1)} %copy-done.8, s32[1,1]{1,0:T(1,128)S(6)} %copy.14.count_ref, f32[3,24,128]{2,1,0:T(8,128)S(1)} %copy-done.1, f32[24,128]{1,0:T(8,128)S(1)} %copy-done.7, f32[3,24,128]{2,1,0:T(8,128)S(1)} %copy-done.6, f32[9,24,128]{2,1,0:T(8,128)S(1)} %copy-done.2, ...), custom_call_target="tpu_custom_call" | custom-call | tf_op jit(solution)/shard_map/particles_to_node_speeds/pallas_call | solution.py:648
  26.1 5.5 %nodes_to_particles.1 = (f32[3,24,128]{2,1,0:T(8,128)}, f32[9,24,128]{2,1,0:T(8,128)}, f32[9,24,128]{2,1,0:T(8,128)}, f32[6,24,128]{2,1,0:T(8,128)}) custom-call(s32[24]{0:T(128)S(1)} %copy-done.8, s32[1,1]{1,0:T(1,128)S(6)} %copy.14.count_ref, f32[2064,128]{1,0:T(8,128)S(1)} %particles_to_node_speeds.1.speed_ref, f32[3,24,128]{2,1,0:T(8,128)S(1)} %copy-done.1, ...), custom_call_target="tpu_custom_call" | custom-call | tf_op jit(solution)/shard_map/nodes_to_particles/pallas_call | solution.py:678
Async XLA Ops:
  1.3 0.9 %copy-start = (f32[9,24,128]{2,1,0:T(8,128)S(1)}, f32[9,24,128]{2,1,0:T(8,128)}, u32[]{:S(2)}) copy-start(f32[9,24,128]{2,1,0:T(8,128)} %deform_ref.1) | copy-start | bytes 331780
  2.2 0.8 %copy-start.1 = (f32[3,24,128]{2,1,0:T(8,128)S(1)}, f32[3,24,128]{2,1,0:T(8,128)}, u32[]{:S(2)}) copy-start(f32[3,24,128]{2,1,0:T(8,128)} %offset_ref.1) | copy-start | bytes 110596
  2.9 0.9 %copy-start.2 = (f32[9,24,128]{2,1,0:T(8,128)S(1)}, f32[9,24,128]{2,1,0:T(8,128)}, u32[]{:S(2)}) copy-start(f32[9,24,128]{2,1,0:T(8,128)} %affine_hbm.1) | copy-start | bytes 331780
  3.8 0.8 %copy-start.3 = (s32[8,8,256]{2,1,0:T(8,128)S(1)}, s32[8,8,256]{2,1,0:T(8,128)}, u32[]{:S(2)}) copy-start(s32[8,8,256]{2,1,0:T(8,128)} %code_hbm.1) | copy-start | bytes 196612
  4.7 0.7 %copy-start.4 = (s32[24,128]{1,0:T(8,128)S(1)}, s32[24,128]{1,0:T(8,128)}, u32[]{:S(2)}) copy-start(s32[24,128]{1,0:T(8,128)} %cell_ref.1) | copy-start | bytes 36868
  5.4 0.7 %copy-start.5 = (s32[24,128]{1,0:T(8,128)S(1)}, s32[24,128]{1,0:T(8,128)}, u32[]{:S(2)}) copy-start(s32[24,128]{1,0:T(8,128)} %body_ref.1) | copy-start | bytes 36868
  6.1 0.8 %copy-start.6 = (f32[3,24,128]{2,1,0:T(8,128)S(1)}, f32[3,24,128]{2,1,0:T(8,128)}, u32[]{:S(2)}) copy-start(f32[3,24,128]{2,1,0:T(8,128)} %velocity_hbm.1) | copy-start | bytes 110596
  6.9 0.7 %copy-start.7 = (f32[24,128]{1,0:T(8,128)S(1)}, f32[24,128]{1,0:T(8,128)}, u32[]{:S(2)}) copy-start(f32[24,128]{1,0:T(8,128)} %mass_hbm.1) | copy-start | bytes 36868
  7.6 0.7 %copy-start.8 = (s32[24]{0:T(128)S(1)}, s32[24]{0:T(128)}, u32[]{:S(2)}) copy-start(s32[24]{0:T(128)} %tile_ref.3) | copy-start | bytes 292

commit v3 on v2

--- a/solution.py
+++ b/solution.py
@@ -141,7 +141,7 @@
     cell_hbm,
     body_hbm,
     code_hbm,
-    speed_ref,
+    result_ref,
     *scratch,
 ):
     n_x, n_y, padded_nodes, halves, tiles, unroll = shape
@@ -160,10 +160,13 @@
         planes_ref,
         send_code,
         recv_code,
-    ) = scratch[8:19]
-    sends = scratch[19:25]
-    recvs = scratch[25:31]
-    send_sem, recv_sem, code_send_sem, code_recv_sem, in_sem, table_sem = scratch[31:]
+        speed_ref,
+        high_ref,
+        low_ref,
+    ) = scratch[8:22]
+    sends = scratch[22:28]
+    recvs = scratch[28:34]
+    send_sem, recv_sem, code_send_sem, code_recv_sem, in_sem, table_sem = scratch[34:]
     blocks = mass_ref.shape[0]
     size_x, size_y = lax.axis_size("gx"), lax.axis_size("gy")
     me_x, me_y = lax.axis_index("gx"), lax.axis_index("gy")
@@ -274,6 +277,8 @@
         right = jnp.concatenate(planes, 1)
         left_high, left_low = split(left)
         right_high, right_low = split(right)
+        high_ref[block] = right_high
+        low_ref[block] = right_low
         product = lax.dot_general(
             jnp.concatenate([left_high, left_low], 0),
             jnp.concatenate([right_high, right_low], 0),
@@ -501,60 +506,23 @@
     update_groups(late, groups - late)
     edge = jnp.zeros((SUB, LANES), F32)
     depth = halves * LANES
-    speed_ref[pl.ds(0, SUB), :] = edge
-    speed_ref[pl.ds((depth + 1) * SUB, SUB), :] = edge
+    grid_ref[pl.ds(0, SUB), :] = edge
+    grid_ref[pl.ds((depth + 1) * SUB, SUB), :] = edge
     for half in range(halves):
         for c in range(6):
             channel = c // 3 * 4 + c % 3
-            speed_ref[
+            grid_ref[
                 pl.ds((1 + half * LANES) * SUB + channel, LANES, stride=SUB), :
             ] = planes_ref[half * 6 + c].T
-        for channel in (3, 7):
-            speed_ref[
-                pl.ds((1 + half * LANES) * SUB + channel, LANES, stride=SUB), :
-            ] = jnp.zeros((LANES, LANES), F32)
-
-    for index in range(8):
-
-        @pl.when(valid[index])
-        def _(index=index):
-            code_copy(index).wait_send()
-
-    for face in range(6):
-
-        @pl.when(face_valid(face))
-        def _(face=face):
-            face_copy(face).wait_send()
-
-
-def gather_kernel(
-    shape,
-    tile_ref,
-    count_ref,
-    speed_ref,
-    offset_ref,
-    deform_ref,
-    cell_ref,
-    body_ref,
-    new_velocity_ref,
-    new_affine_ref,
-    new_deform_ref,
-    new_stress_ref,
-    result_ref,
-    rows_ref,
-):
-    n_x, padded_nodes, tiles, unroll = shape
-    blocks = cell_ref.shape[0]
-    store_rows(rows_ref, blocks, offset_ref, cell_ref)
-    coordinates = node_coordinates(n_x, padded_nodes)
+    for j in range(tiles[1]):
+        speed_ref[j] = grid_ref[pl.ds(j * body_rows, body_rows), :]
+    speed_ref[tiles[1], pl.ds(0, over), :] = grid_ref[pl.ds(tiles[1] * body_rows, over), :]
 
     def block_speeds(block):
-        tile = tile_ref[block]
-        planes = plane_weights(rows_ref, blocks, block, tile, tiles, coordinates)
-        start = pl.multiple_of(tile % tiles[1] * (TILE_Z * SUB), SUB)
-        speeds = speed_ref[pl.ds(start, SPAN_Z * SUB), :]
+        at = tile_ref[block] % tiles[1]
+        speeds = jnp.concatenate([speed_ref[at], speed_ref[at + 1][:over]], 0)
         left_high, left_low = split(speeds)
-        right_high, right_low = split(jnp.concatenate(planes, 1))
+        right_high, right_low = high_ref[block], low_ref[block]
         product = jnp.dot(
             jnp.concatenate([left_high, left_low, left_high], 1),
             jnp.concatenate([right_high, right_high, right_low], 0),
@@ -571,7 +539,7 @@
             sums[3] = sums[3] + rows[0] * moment
         return sums
 
-    def step(index, carry):
+    def gather_step(index, carry):
         members = [index * unroll + u for u in range(unroll)]
         results = [block_speeds(block) for block in members]
         for block, sums in zip(members, results):
@@ -580,8 +548,61 @@
                 result_ref[pl.ds(start, SUB), :] = sums[v]
         return carry
 
-    lax.fori_loop(0, blocks // unroll, step, 0)
-    slot = lax.broadcasted_iota(jnp.int32, cell_ref.shape, 0)
+    lax.fori_loop(0, blocks // unroll, gather_step, 0)
+
+    for index in range(8):
+
+        @pl.when(valid[index])
+        def _(index=index):
+            code_copy(index).wait_send()
+
+    for face in range(6):
+
+        @pl.when(face_valid(face))
+        def _(face=face):
+            face_copy(face).wait_send()
+
+
+def particle_kernel(
+    count_ref,
+    result_hbm,
+    deform_hbm,
+    body_hbm,
+    new_velocity_hbm,
+    new_affine_hbm,
+    new_deform_hbm,
+    new_stress_hbm,
+    result_ref,
+    deform_ref,
+    body_ref,
+    new_velocity_ref,
+    new_affine_ref,
+    new_deform_ref,
+    new_stress_ref,
+    in_sem,
+    out_sem,
+):
+    pairs = ((result_hbm, result_ref), (deform_hbm, deform_ref), (body_hbm, body_ref))
+    loads = [
+        pltpu.make_async_copy(source, target, in_sem.at[i])
+        for i, (source, target) in enumerate(pairs)
+    ]
+    for load in loads:
+        load.start()
+    pairs = (
+        (new_velocity_ref, new_velocity_hbm),
+        (new_affine_ref, new_affine_hbm),
+        (new_deform_ref, new_deform_hbm),
+        (new_stress_ref, new_stress_hbm),
+    )
+    stores = [
+        pltpu.make_async_copy(source, target, out_sem.at[i])
+        for i, (source, target) in enumerate(pairs)
+    ]
+    for load in loads:
+        load.wait()
+    blocks = body_ref.shape[0]
+    slot = lax.broadcasted_iota(jnp.int32, body_ref.shape, 0)
     live = slot < count_ref[0, 0]
     even = body_ref[...] % 2 == 0
 
@@ -594,6 +615,7 @@
 
     for r in range(3):
         new_velocity_ref[r] = take(0, r)
+    stores[0].start()
     affine = [4.0 * take(1 + c, r) for r in range(3) for c in range(3)]
     deform = [deform_ref[i] for i in range(9)]
     moved = []
@@ -605,9 +627,15 @@
             moved.append(jnp.where(live, entry, 0.0))
     for i in range(9):
         new_affine_ref[i] = affine[i]
+    stores[1].start()
+    for i in range(9):
         new_deform_ref[i] = moved[i]
+    stores[2].start()
     for i, entry in enumerate(kirchhoff(moved)):
         new_stress_ref[i] = jnp.where(live, entry, 0.0)
+    stores[3].start()
+    for store in stores:
+        store.wait()
 
 
 def per_device(
@@ -633,9 +661,8 @@
     assert own_x == own_y and max(blocks, tiles[1]) <= LANES
     vmem = pl.BlockSpec(memory_space=pltpu.VMEM)
     smem = pl.BlockSpec(memory_space=pltpu.SMEM)
-    limit = 40 * 1024 * 1024
-    grid_shape = jax.ShapeDtypeStruct(((depth + 2) * SUB, LANES), F32)
-    work = (n_x, padded_nodes, tiles, unroll)
+    hbm = pl.BlockSpec(memory_space=pltpu.HBM)
+    result_shape = jax.ShapeDtypeStruct((4 * blocks * SUB, LANES), F32)
     operands = (offset, particle_mass, velocity, affine, deform, particle_cell, body_id)
     operands = operands + (normal_code,)
     faces = [
@@ -645,19 +672,19 @@
         for face in FACES
     ]
     dma = pltpu.SemaphoreType.DMA
-    speeds = pl.pallas_call(
+    result = pl.pallas_call(
         functools.partial(
             nodes_kernel, (n_x, n_y, padded_nodes, halves, tiles, unroll)
         ),
-        out_shape=grid_shape,
-        in_specs=[smem, smem] + [pl.BlockSpec(memory_space=pltpu.HBM)] * 8,
+        out_shape=result_shape,
+        in_specs=[smem, smem] + [hbm] * 8,
         out_specs=vmem,
         scratch_shapes=[pltpu.VMEM(a.shape, a.dtype) for a in operands]
         + [
             pltpu.VMEM((4 * blocks * SUB, LANES), F32),
             pltpu.VMEM((N_ROWS * blocks, LANES), F32),
             pltpu.VMEM((blocks + 1, SPAN_Z * SUB, LANES), F32),
-            pltpu.VMEM(grid_shape.shape, F32),
+            pltpu.VMEM(((depth + 2) * SUB, LANES), F32),
             pltpu.VMEM((SUB, LANES), jnp.int32),
             pltpu.SMEM((SUB, LANES), jnp.int32),
             pltpu.VMEM((halves * padded_nodes * SUB, LANES), F32),
@@ -665,28 +692,31 @@
             pltpu.VMEM((halves * 6, LANES, LANES), F32),
             pltpu.VMEM((8, halves * own_y, LANES), jnp.int32),
             pltpu.VMEM((8, halves * own_y, LANES), jnp.int32),
+            pltpu.VMEM((tiles[1] + 1, TILE_Z * SUB, LANES), F32),
+            pltpu.VMEM((blocks, LANES, 3 * LANES), BF16),
+            pltpu.VMEM((blocks, LANES, 3 * LANES), BF16),
         ]
         + faces
         + faces
         + [dma((6,)), dma((6,)), dma((8,)), dma((8,)), dma((8,)), dma(())],
-        compiler_params=pltpu.CompilerParams(
-            collective_id=0, has_side_effects=True, vmem_limit_bytes=limit
-        ),
-        name="particles_to_node_speeds",
+        compiler_params=pltpu.CompilerParams(collective_id=0, has_side_effects=True),
+        name="nodes_step",
     )(slot_tile_number, block_count, *operands)
-    shaped = lambda n: jax.ShapeDtypeStruct((n, blocks, LANES), F32)
+    shapes = [jax.ShapeDtypeStruct((n, blocks, LANES), F32) for n in (3, 9, 9, 6)]
     return pl.pallas_call(
-        functools.partial(gather_kernel, work),
-        out_shape=(shaped(3), shaped(9), shaped(9), shaped(6)),
-        in_specs=[smem, smem] + [vmem] * 5,
-        out_specs=(vmem,) * 4,
+        particle_kernel,
+        out_shape=tuple(shapes),
+        in_specs=[smem] + [hbm] * 3,
+        out_specs=(hbm,) * 4,
         scratch_shapes=[
-            pltpu.VMEM((4 * blocks * SUB, LANES), F32),
-            pltpu.VMEM((N_ROWS * blocks, LANES), F32),
-        ],
-        compiler_params=pltpu.CompilerParams(vmem_limit_bytes=limit),
-        name="nodes_to_particles",
-    )(slot_tile_number, block_count, speeds, offset, deform, particle_cell, body_id)
+            pltpu.VMEM(result_shape.shape, F32),
+            pltpu.VMEM(deform.shape, F32),
+            pltpu.VMEM(body_id.shape, jnp.int32),
+        ]
+        + [pltpu.VMEM(a.shape, F32) for a in shapes]
+        + [dma((3,)), dma((4,))],
+        name="particles_step",
+    )(block_count, result, deform, body_id)
 
 
 def solution(mesh):

time: 32.1 us -> 25 us (0.78); the launches traced: 31.6 us -> 24.8 us
  local copies, waits for them, and re-layouts: 6.93 us -> 0 us
    unnamed x18 -> x0, local copies, waits for them, and re-layouts: 6.93 us -> none
    pallas_call x1, Pallas kernels: 17.8 us -> 21.7 us  [per_device(): pl.pallas_call(functools.partial(nodes_kernel, (n_x, n_y, padded_nodes, h...]
    pallas_call x1, Pallas kernels: 5.49 us -> 1.86 us  [per_device(): pl.pallas_call(particle_kernel, out_shape=tuple(shapes), in_specs=[smem]...]
where the time goes in v3:
time: 25 us; the launch traced here: 24.8 us
  Pallas kernels  23.6 us (94%)
  between operations  1.29 us (5%)
    pallas_call x1, Pallas kernels, per_device(): pl.pallas_call(functools.partial(nodes_kernel, (n_x, n_y, padded_nodes, h...  21.7 us
    pallas_call x1, Pallas kernels, per_device(): pl.pallas_call(particle_kernel, out_shape=tuple(shapes), in_specs=[smem]...  1.86 us

profile of v3, /device:TPU:13, one launch (start us, length us, event | category | flops | bytes accessed | tf_op | source)
XLA Modules:
  0.0 24.8 jit_solution(7022979864522141438)
XLA Ops:
  1.3 21.7 %nodes_step.1.result_hbm = f32[768,128]{1,0:T(8,128)} custom-call(s32[24]{0:T(128)} %tile_ref.1, s32[1,1]{1,0:T(1,128)S(6)} %copy.14.count_ref, f32[3,24,128]{2,1,0:T(8,128)} %offset_hbm.1, f32[24,128]{1,0:T(8,128)} %mass_hbm.1, f32[3,24,128]{2,1,0:T(8,128)} %velocity_hbm.1, f32[9,24,128]{2,1,0:T(8,128)} %affine_hbm.1, f32[9,24,128]{2,1,0:T(8,128)} %deform_hbm.3, ...), custom_call_target="tpu_custom_call" | custom-call | tf_op jit(solution)/shard_map/nodes_step/pallas_call | solution.py:675
  23.0 1.9 %particles_step.1 = (f32[3,24,128]{2,1,0:T(8,128)}, f32[9,24,128]{2,1,0:T(8,128)}, f32[9,24,128]{2,1,0:T(8,128)}, f32[6,24,128]{2,1,0:T(8,128)}) custom-call(s32[1,1]{1,0:T(1,128)S(6)} %copy.14.count_ref, f32[768,128]{1,0:T(8,128)} %nodes_step.1.result_hbm, f32[9,24,128]{2,1,0:T(8,128)} %deform_hbm.3, s32[24,128]{1,0:T(8,128)} %body_hbm.3), custom_call_target="tpu_custom_call" | custom-call | tf_op jit(solution)/shard_map/particles_step/pallas_call | solution.py:706

commit v4 on v3

--- a/solution.py
+++ b/solution.py
@@ -657,7 +657,7 @@
     padded_nodes = -(-n_x * n_y // SUB) * SUB
     halves = depth // LANES
     assert particles == LANES and padded_nodes <= LANES and depth % LANES == 0
-    unroll = 2 if blocks % 2 == 0 else 1
+    unroll = next(u for u in (8, 4, 2, 1) if blocks % u == 0)
     assert own_x == own_y and max(blocks, tiles[1]) <= LANES
     vmem = pl.BlockSpec(memory_space=pltpu.VMEM)
     smem = pl.BlockSpec(memory_space=pltpu.SMEM)

time: 25 us -> 22.3 us (0.89)
  Pallas kernels: 23.6 us -> 20.8 us
    pallas_call x1, Pallas kernels: 21.7 us -> 19 us  [per_device(): pl.pallas_call(functools.partial(nodes_kernel, (n_x, n_y, padded_nodes, h...]
where the time goes in v4:
time: 22.3 us; the launch traced here: 22.1 us
  Pallas kernels  20.8 us (93%)
  between operations  1.29 us (6%)
    pallas_call x1, Pallas kernels, per_device(): pl.pallas_call(functools.partial(nodes_kernel, (n_x, n_y, padded_nodes, h...  19 us
    pallas_call x1, Pallas kernels, per_device(): pl.pallas_call(particle_kernel, out_shape=tuple(shapes), in_specs=[smem]...  1.86 us

profile of v4, /device:TPU:13, one launch (start us, length us, event | category | flops | bytes accessed | tf_op | source)
XLA Modules:
  0.0 22.1 jit_solution(782060450486568239)
XLA Ops:
  1.3 19.0 %nodes_step.1.result_hbm = f32[768,128]{1,0:T(8,128)} custom-call(s32[24]{0:T(128)} %tile_ref.1, s32[1,1]{1,0:T(1,128)S(6)} %copy.14.count_ref, f32[3,24,128]{2,1,0:T(8,128)} %offset_hbm.1, f32[24,128]{1,0:T(8,128)} %mass_hbm.1, f32[3,24,128]{2,1,0:T(8,128)} %velocity_hbm.1, f32[9,24,128]{2,1,0:T(8,128)} %affine_hbm.1, f32[9,24,128]{2,1,0:T(8,128)} %deform_hbm.3, ...), custom_call_target="tpu_custom_call" | custom-call | tf_op jit(solution)/shard_map/nodes_step/pallas_call | solution.py:675
  20.3 1.9 %particles_step.1 = (f32[3,24,128]{2,1,0:T(8,128)}, f32[9,24,128]{2,1,0:T(8,128)}, f32[9,24,128]{2,1,0:T(8,128)}, f32[6,24,128]{2,1,0:T(8,128)}) custom-call(s32[1,1]{1,0:T(1,128)S(6)} %copy.14.count_ref, f32[768,128]{1,0:T(8,128)} %nodes_step.1.result_hbm, f32[9,24,128]{2,1,0:T(8,128)} %deform_hbm.3, s32[24,128]{1,0:T(8,128)} %body_hbm.3), custom_call_target="tpu_custom_call" | custom-call | tf_op jit(solution)/shard_map/particles_step/pallas_call | solution.py:706

commit v5 on v4

--- a/solution.py
+++ b/solution.py
@@ -87,33 +87,67 @@
 N_ROWS = 14 + 2 * SPAN_Z
 
 
-def node_coordinates(n_x, padded_nodes):
-    node = lax.broadcasted_iota(jnp.int32, (padded_nodes, LANES), 0)
-    return (node % n_x).astype(F32), (node // n_x).astype(F32)
-
-
-def plane_weights(rows_ref, blocks, block, tile, tiles, coordinates):
+def plane_groups(n_x, n_y):
+    groups = [(n_x + x, n_x) for x in range(n_x)]
+    groups += [(0, 1), ((n_y - 1) * n_x, 1)]
+    corners = [(SUB, 0), (SUB + 1, 0), (SUB, n_y - 1), (SUB + 1, n_y - 1)]
+    return groups, [y * n_x + x for x, y in corners]
+
+
+def axis_weights(rows_ref, blocks, block, axis, corner, coordinates):
+    def row(index):
+        return rows_ref[pl.ds((7 * axis + index) * blocks + block, 1), :]
+
+    base = row(0) + corner
+    weights = [row(1 + s) for s in range(3)]
+    moments = [row(4 + s) for s in range(3)]
+    out = []
+    for coordinate in coordinates:
+        step = coordinate - base
+        hits = [step == float(s) for s in range(3)]
+        for rows in (weights, moments):
+            total = jnp.zeros_like(step)
+            for s in range(3):
+                total = jnp.where(hits[s], rows[s], total)
+            out.append(total)
+    return out
+
+
+def plane_weights(rows_ref, blocks, block, tile, tiles, n_x, n_y):
     tiles_y, tiles_z = tiles
     tile_x = (tile // (tiles_y * tiles_z) * TILE_X).astype(F32)
     tile_y = (tile // tiles_z % tiles_y * TILE_Y).astype(F32)
-
-    def row(index):
-        return rows_ref[pl.ds(index * blocks + block, 1), :]
-
-    parts = []
-    for axis, corner in enumerate((tile_x, tile_y)):
-        first = 7 * axis
-        step = coordinates[axis] - (row(first) + corner)
-        hits = [step == float(s) for s in range(3)]
-        for shift in (1, 4):
-            total = jnp.zeros_like(step)
-            for s in range(3):
-                total = jnp.where(hits[s], row(first + shift + s), total)
-            parts.append(total)
-    weight_x, moment_x, weight_y, moment_y = parts
-    out = [weight_x * weight_y, moment_x * weight_y, weight_x * moment_y]
-    pad = jnp.zeros((LANES - coordinates[0].shape[0], LANES), F32)
-    return [jnp.concatenate([p, pad], 0) for p in out]
+    lines = lax.broadcasted_iota(jnp.int32, (SUB, LANES), 0)
+    low_x = lines.astype(F32)
+    high_x = (lines % 2 + SUB).astype(F32)
+    inner_y = low_x + 1.0
+    outer_y = jnp.where(lines % 4 < 2, 0, n_y - 1).astype(F32)
+    wx, mx, wx_high, mx_high = axis_weights(
+        rows_ref, blocks, block, 0, tile_x, (low_x, high_x)
+    )
+    wy, my, wy_outer, my_outer = axis_weights(
+        rows_ref, blocks, block, 1, tile_y, (inner_y, outer_y)
+    )
+
+    def line(low, high, x):
+        value = low[x : x + 1] if x < SUB else high[x - SUB : x - SUB + 1]
+        return jnp.broadcast_to(value, (SUB, LANES))
+
+    weight_x = [line(wx, wx_high, x) for x in range(n_x)]
+    moment_x = [line(mx, mx_high, x) for x in range(n_x)]
+    first = [jnp.broadcast_to(v[0:1], (SUB, LANES)) for v in (wy_outer, my_outer)]
+    last = [jnp.broadcast_to(v[2:3], (SUB, LANES)) for v in (wy_outer, my_outer)]
+    corner = lines < 4
+    wx_high = jnp.where(corner, wx_high, 0.0)
+    mx_high = jnp.where(corner, mx_high, 0.0)
+    pairs = [(weight_x[x], moment_x[x], wy, my) for x in range(n_x)]
+    pairs += [(wx, mx, *first), (wx, mx, *last), (wx_high, mx_high, wy_outer, my_outer)]
+    pad = [jnp.zeros((LANES - SUB * len(pairs), LANES), F32)]
+    return [
+        jnp.concatenate([w * v for w, _, v, _ in pairs] + pad, 0),
+        jnp.concatenate([m * v for _, m, v, _ in pairs] + pad, 0),
+        jnp.concatenate([w * n for w, _, _, n in pairs] + pad, 0),
+    ]
 
 
 def face_runs(kind, side, n_x, n_y):
@@ -252,14 +286,13 @@
             for r in range(3):
                 put(1 + c, 4 * field + 1 + r, masses[field] * force[3 * r + c])
     store_rows(rows_ref, blocks, offset_ref, cell_ref)
-    coordinates = node_coordinates(n_x, padded_nodes)
     span = SPAN_Z * SUB
     chain_ref[0] = jnp.zeros((span, LANES), F32)
     table_copy.wait()
 
     def block_sums(block):
         tile = tile_ref[block]
-        planes = plane_weights(rows_ref, blocks, block, tile, tiles, coordinates)
+        planes = plane_weights(rows_ref, blocks, block, tile, tiles, n_x, n_y)
         groups = [
             source_ref[
                 pl.ds(pl.multiple_of(g * blocks * SUB + block * SUB, SUB), SUB), :
@@ -363,12 +396,25 @@
     tail = lax.fori_loop(0, tiles[1], assemble, jnp.zeros((over, LANES), F32), unroll=4)
     grid_ref[pl.ds(tiles[1] * body_rows, over), :] = tail
 
+    lane_groups, lane_corners = plane_groups(n_x, n_y)
+    nodes = n_x * n_y
+
     for half in range(halves):
         for c in range(SUB):
             part = grid_ref[pl.ds((1 + half * LANES) * SUB + c, LANES, stride=SUB), :]
-            node_ref[pl.ds(half * plane + c, padded_nodes, stride=SUB), :] = part.T[
-                :padded_nodes
-            ]
+            part = part.T
+            for i, (first, hop) in enumerate(lane_groups):
+                node_ref[
+                    pl.ds(half * plane + first * SUB + c, SUB, stride=hop * SUB), :
+                ] = part[i * SUB : (i + 1) * SUB]
+            at = len(lane_groups) * SUB
+            for i, first in enumerate(lane_corners):
+                node_ref[pl.ds(half * plane + first * SUB + c, 1), :] = part[
+                    at + i : at + i + 1
+                ]
+            node_ref[
+                pl.ds(half * plane + nodes * SUB + c, padded_nodes - nodes, stride=SUB), :
+            ] = jnp.zeros((padded_nodes - nodes, LANES), F32)
 
     def each_run(face):
         offset = 0
@@ -410,9 +456,6 @@
             codes_ref[
                 pl.ds(half * padded_nodes + n_x + x + 1, own_y, stride=n_x), :
             ] = code_ref[x, :, lanes]
-    planes_ref[:, pl.ds(padded_nodes, LANES - padded_nodes), :] = jnp.zeros(
-        (planes_ref.shape[0], LANES - padded_nodes, LANES), F32
-    )
     for index, (dx, dy) in enumerate(DIRECTIONS):
 
         @pl.when(valid[index])
@@ -484,11 +527,11 @@
         x = me_x * own_x + node % n_x
         y = me_y * own_y + node // n_x
         inside = (x >= 1) & (x <= size_x * own_x) & (y >= 1) & (y <= size_y * own_y)
-        rows = pl.ds(pl.multiple_of(group * SUB, SUB), SUB)
         for f, sign in ((0, -1.0), (1, 1.0)):
             for r in range(3):
                 speed = speeds[f][r] + sign * closing[f] * normal[r]
-                planes_ref[half * 6 + 3 * f + r, rows, :] = jnp.where(inside, speed, 0.0)
+                at = (half * 6 + 3 * f + r) * LANES + pl.multiple_of(group * SUB, SUB)
+                planes_ref[pl.ds(at, SUB), :] = jnp.where(inside, speed, 0.0)
 
     def update_groups(first, count):
         def body(step, carry):
@@ -511,9 +554,17 @@
     for half in range(halves):
         for c in range(6):
             channel = c // 3 * 4 + c % 3
+            at = (half * 6 + c) * LANES
+            part = [
+                planes_ref[pl.ds(at + first, SUB, stride=hop), :]
+                for first, hop in lane_groups
+            ]
+            part += [planes_ref[pl.ds(at + first, 1), :] for first in lane_corners]
+            rest = LANES - len(lane_groups) * SUB - len(lane_corners)
+            part.append(jnp.zeros((rest, LANES), F32))
             grid_ref[
                 pl.ds((1 + half * LANES) * SUB + channel, LANES, stride=SUB), :
-            ] = planes_ref[half * 6 + c].T
+            ] = jnp.concatenate(part, 0).T
     for j in range(tiles[1]):
         speed_ref[j] = grid_ref[pl.ds(j * body_rows, body_rows), :]
     speed_ref[tiles[1], pl.ds(0, over), :] = grid_ref[pl.ds(tiles[1] * body_rows, over), :]
@@ -657,8 +708,8 @@
     padded_nodes = -(-n_x * n_y // SUB) * SUB
     halves = depth // LANES
     assert particles == LANES and padded_nodes <= LANES and depth % LANES == 0
-    unroll = next(u for u in (8, 4, 2, 1) if blocks % u == 0)
-    assert own_x == own_y and max(blocks, tiles[1]) <= LANES
+    unroll = next(u for u in (24, 8, 4, 2, 1) if blocks % u == 0)
+    assert own_x == own_y == SUB and max(blocks, tiles[1]) <= LANES
     vmem = pl.BlockSpec(memory_space=pltpu.VMEM)
     smem = pl.BlockSpec(memory_space=pltpu.SMEM)
     hbm = pl.BlockSpec(memory_space=pltpu.HBM)
@@ -689,7 +740,7 @@
             pltpu.SMEM((SUB, LANES), jnp.int32),
             pltpu.VMEM((halves * padded_nodes * SUB, LANES), F32),
             pltpu.VMEM((halves * padded_nodes, LANES), jnp.int32),
-            pltpu.VMEM((halves * 6, LANES, LANES), F32),
+            pltpu.VMEM((halves * 6 * LANES, LANES), F32),
             pltpu.VMEM((8, halves * own_y, LANES), jnp.int32),
             pltpu.VMEM((8, halves * own_y, LANES), jnp.int32),
             pltpu.VMEM((tiles[1] + 1, TILE_Z * SUB, LANES), F32),

time: 22.3 us -> 21.1 us (0.946)
  Pallas kernels: 20.8 us -> 19.6 us
    pallas_call x1, Pallas kernels: 19 us -> 17.8 us  [per_device(): pl.pallas_call(functools.partial(nodes_kernel, (n_x, n_y, padded_nodes, h...]
where the time goes in v5:
time: 21.1 us; the launch traced here: 20.9 us
  Pallas kernels  19.6 us (93%)
  between operations  1.29 us (6%)
    pallas_call x1, Pallas kernels, per_device(): pl.pallas_call(functools.partial(nodes_kernel, (n_x, n_y, padded_nodes, h...  17.8 us
    pallas_call x1, Pallas kernels, per_device(): pl.pallas_call(particle_kernel, out_shape=tuple(shapes), in_specs=[smem]...  1.86 us

profile of v5, /device:TPU:13, one launch (start us, length us, event | category | flops | bytes accessed | tf_op | source)
XLA Modules:
  0.0 20.9 jit_solution(15560749760569651184)
XLA Ops:
  1.3 17.8 %nodes_step.1.result_hbm = f32[768,128]{1,0:T(8,128)} custom-call(s32[24]{0:T(128)} %tile_ref.1, s32[1,1]{1,0:T(1,128)S(6)} %copy.14.count_ref, f32[3,24,128]{2,1,0:T(8,128)} %offset_hbm.1, f32[24,128]{1,0:T(8,128)} %mass_hbm.1, f32[3,24,128]{2,1,0:T(8,128)} %velocity_hbm.1, f32[9,24,128]{2,1,0:T(8,128)} %affine_hbm.1, f32[9,24,128]{2,1,0:T(8,128)} %deform_hbm.3, ...), custom_call_target="tpu_custom_call" | custom-call | tf_op jit(solution)/shard_map/nodes_step/pallas_call | solution.py:726
  19.1 1.9 %particles_step.1 = (f32[3,24,128]{2,1,0:T(8,128)}, f32[9,24,128]{2,1,0:T(8,128)}, f32[9,24,128]{2,1,0:T(8,128)}, f32[6,24,128]{2,1,0:T(8,128)}) custom-call(s32[1,1]{1,0:T(1,128)S(6)} %copy.14.count_ref, f32[768,128]{1,0:T(8,128)} %nodes_step.1.result_hbm, f32[9,24,128]{2,1,0:T(8,128)} %deform_hbm.3, s32[24,128]{1,0:T(8,128)} %body_hbm.3), custom_call_target="tpu_custom_call" | custom-call | tf_op jit(solution)/shard_map/particles_step/pallas_call | solution.py:757

commit v6 on v5

--- a/solution.py
+++ b/solution.py
@@ -200,7 +200,9 @@
     ) = scratch[8:22]
     sends = scratch[22:28]
     recvs = scratch[28:34]
-    send_sem, recv_sem, code_send_sem, code_recv_sem, in_sem, table_sem = scratch[34:]
+    send_sem, recv_sem, code_send_sem, code_recv_sem, in_sem, table_sem = scratch[34:40]
+    relays = scratch[40:42]
+    relay_send_sem, relay_recv_sem, pass_send_sem, pass_recv_sem = scratch[42:]
     blocks = mass_ref.shape[0]
     size_x, size_y = lax.axis_size("gx"), lax.axis_size("gy")
     me_x, me_y = lax.axis_index("gx"), lax.axis_index("gy")
@@ -245,6 +247,15 @@
             pl.semaphore_signal(
                 barrier, inc=1, device_id=target(index), device_id_type=MESH
             )
+
+    relayed = size_y == 4
+    if relayed:
+        pl.semaphore_signal(
+            barrier,
+            inc=1,
+            device_id={"gx": me_x, "gy": (me_y + 2) % 4},
+            device_id_type=MESH,
+        )
 
     opposite = [DIRECTIONS.index((-dx, -dy)) for dx, dy in DIRECTIONS]
     plane = padded_nodes * SUB
@@ -371,7 +382,49 @@
     def face_valid(face):
         return valid[min(face, 2 + face % 2)]
 
-    arrivals = sum(ok.astype(jnp.int32) for ok in valid)
+    def is_relayed(face):
+        return me_y == (1 if FACES[face][1] > 0 else 2)
+
+    def is_direct(face):
+        if relayed and face >= 2:
+            return jnp.logical_and(face_valid(face), jnp.logical_not(is_relayed(face)))
+        return face_valid(face)
+
+    def half_rows(ref, half):
+        count = ref.shape[0] // 2
+        return ref.at[pl.ds(half * count, count)]
+
+    def relay_copy(face, half):
+        part, slot = face // 2 - 1, 1 - face % 2
+        return pltpu.make_async_remote_copy(
+            src_ref=half_rows(sends[face], half),
+            dst_ref=relays[part].at[slot],
+            send_sem=relay_send_sem.at[2 * part + half],
+            recv_sem=relay_recv_sem.at[2 * part + slot],
+            device_id={"gx": me_x, "gy": 3 * half},
+            device_id_type=MESH,
+        )
+
+    def pass_copy(part, slot, half):
+        return pltpu.make_async_remote_copy(
+            src_ref=relays[part].at[slot],
+            dst_ref=half_rows(recvs[2 * part + 2 + slot], half),
+            send_sem=pass_send_sem.at[2 * part + slot],
+            recv_sem=pass_recv_sem.at[2 * part + half],
+            device_id={"gx": me_x, "gy": 2 - slot},
+            device_id_type=MESH,
+        )
+
+    def pass_on(part):
+        for half in range(2):
+
+            @pl.when(me_y == 3 * half)
+            def _(half=half):
+                for slot in range(2):
+                    relay_copy(2 * part + 3 - slot, half).wait_recv()
+                    pass_copy(part, slot, half).start()
+
+    arrivals = sum(ok.astype(jnp.int32) for ok in valid) + int(relayed)
     pl.semaphore_wait(barrier, arrivals)
     for index in range(8):
 
@@ -426,11 +479,22 @@
                 )
                 offset += count * SUB
 
+    def send_far(face):
+        for rows, run in each_run(face):
+            sends[face][run, :] = node_ref[rows, :]
+        if relayed:
+
+            @pl.when(is_relayed(face))
+            def _():
+                for half in range(2):
+                    relay_copy(face, half).start()
+
     def send_face(face):
-        for nodes, run in each_run(face):
-            sends[face][run, :] = node_ref[nodes, :]
-
-        @pl.when(face_valid(face))
+        if face < 2:
+            for rows, run in each_run(face):
+                sends[face][run, :] = node_ref[rows, :]
+
+        @pl.when(is_direct(face))
         def _():
             face_copy(face).start()
 
@@ -439,14 +503,23 @@
             recvs[face][...] = jnp.zeros_like(recvs[face])
 
     def take_face(face):
-        @pl.when(face_valid(face))
+        @pl.when(is_direct(face))
         def _():
             face_copy(face ^ 1).wait_recv()
 
-        for nodes, run in each_run(face):
-            node_ref[nodes, :] = node_ref[nodes, :] + recvs[face][run, :]
-
-    for face in (0, 1, 2, 3):
+        if relayed and face >= 2:
+
+            @pl.when(is_relayed(face))
+            def _():
+                for half in range(2):
+                    pass_copy(face // 2 - 1, face % 2, half).wait_recv()
+
+        for rows, run in each_run(face):
+            node_ref[rows, :] = node_ref[rows, :] + recvs[face][run, :]
+
+    send_far(2)
+    send_far(3)
+    for face in (2, 3, 0, 1):
         send_face(face)
 
     codes_ref[...] = jnp.zeros_like(codes_ref)
@@ -480,8 +553,12 @@
                     index, pl.ds(half * own_y, 1), :
                 ]
 
+    if relayed:
+        pass_on(0)
     take_face(0)
     take_face(1)
+    send_far(4)
+    send_far(5)
     send_face(4)
     send_face(5)
 
@@ -543,6 +620,8 @@
     early = -(-2 * n_x // SUB)
     late = (n_y - 2) * n_x // SUB
     update_groups(early, late - early)
+    if relayed:
+        pass_on(1)
     for face in (2, 3, 4, 5):
         take_face(face)
     update_groups(0, early)
@@ -609,9 +688,25 @@
 
     for face in range(6):
 
-        @pl.when(face_valid(face))
+        @pl.when(is_direct(face))
         def _(face=face):
             face_copy(face).wait_send()
+
+        if relayed and face >= 2:
+
+            @pl.when(is_relayed(face))
+            def _(face=face):
+                for half in range(2):
+                    relay_copy(face, half).wait_send()
+
+    if relayed:
+        for half in range(2):
+
+            @pl.when(me_y == 3 * half)
+            def _(half=half):
+                for part in range(2):
+                    for slot in range(2):
+                        pass_copy(part, slot, half).wait_send()
 
 
 def particle_kernel(
@@ -749,7 +844,9 @@
         ]
         + faces
         + faces
-        + [dma((6,)), dma((6,)), dma((8,)), dma((8,)), dma((8,)), dma(())],
+        + [dma((6,)), dma((6,)), dma((8,)), dma((8,)), dma((8,)), dma(())]
+        + [pltpu.VMEM((2, face.shape[0] // 2, LANES), F32) for face in faces[2::2]]
+        + [dma((4,))] * 4,
         compiler_params=pltpu.CompilerParams(collective_id=0, has_side_effects=True),
         name="nodes_step",
     )(slot_tile_number, block_count, *operands)

time: 21.1 us -> 20.9 us (level)
  Pallas kernels: 19.6 us -> 19.3 us
    pallas_call x1, Pallas kernels: 17.8 us -> 17.5 us  [per_device(): pl.pallas_call(functools.partial(nodes_kernel, (n_x, n_y, padded_nodes, h...]
where the time goes in v6:
time: 20.9 us; the launch traced here: 20.6 us
  Pallas kernels  19.3 us (92%)
  between operations  1.29 us (6%)
    pallas_call x1, Pallas kernels, per_device(): pl.pallas_call(functools.partial(nodes_kernel, (n_x, n_y, padded_nodes, h...  17.5 us
    pallas_call x1, Pallas kernels, per_device(): pl.pallas_call(particle_kernel, out_shape=tuple(shapes), in_specs=[smem]...  1.86 us

profile of v6, /device:TPU:13, one launch (start us, length us, event | category | flops | bytes accessed | tf_op | source)
XLA Modules:
  0.0 20.6 jit_solution(12389924199891200473)
XLA Ops:
  1.3 17.5 %nodes_step.1.result_hbm = f32[768,128]{1,0:T(8,128)} custom-call(s32[24]{0:T(128)} %tile_ref.1, s32[1,1]{1,0:T(1,128)S(6)} %copy.14.count_ref, f32[3,24,128]{2,1,0:T(8,128)} %offset_hbm.1, f32[24,128]{1,0:T(8,128)} %mass_hbm.1, f32[3,24,128]{2,1,0:T(8,128)} %velocity_hbm.1, f32[9,24,128]{2,1,0:T(8,128)} %affine_hbm.1, f32[9,24,128]{2,1,0:T(8,128)} %deform_hbm.3, ...), custom_call_target="tpu_custom_call" | custom-call | tf_op jit(solution)/shard_map/nodes_step/pallas_call | solution.py:821
  18.7 1.9 %particles_step.1 = (f32[3,24,128]{2,1,0:T(8,128)}, f32[9,24,128]{2,1,0:T(8,128)}, f32[9,24,128]{2,1,0:T(8,128)}, f32[6,24,128]{2,1,0:T(8,128)}) custom-call(s32[1,1]{1,0:T(1,128)S(6)} %copy.14.count_ref, f32[768,128]{1,0:T(8,128)} %nodes_step.1.result_hbm, f32[9,24,128]{2,1,0:T(8,128)} %deform_hbm.3, s32[24,128]{1,0:T(8,128)} %body_hbm.3), custom_call_target="tpu_custom_call" | custom-call | tf_op jit(solution)/shard_map/particles_step/pallas_call | solution.py:854

commit v7 on v6

--- a/solution.py
+++ b/solution.py
@@ -175,7 +175,7 @@
     cell_hbm,
     body_hbm,
     code_hbm,
-    result_ref,
+    chosen_ref,
     *scratch,
 ):
     n_x, n_y, padded_nodes, halves, tiles, unroll = shape
@@ -197,12 +197,13 @@
         speed_ref,
         high_ref,
         low_ref,
-    ) = scratch[8:22]
-    sends = scratch[22:28]
-    recvs = scratch[28:34]
-    send_sem, recv_sem, code_send_sem, code_recv_sem, in_sem, table_sem = scratch[34:40]
-    relays = scratch[40:42]
-    relay_send_sem, relay_recv_sem, pass_send_sem, pass_recv_sem = scratch[42:]
+        result_ref,
+    ) = scratch[8:23]
+    sends = scratch[23:29]
+    recvs = scratch[29:35]
+    send_sem, recv_sem, code_send_sem, code_recv_sem, in_sem, table_sem = scratch[35:41]
+    relays = scratch[41:43]
+    relay_send_sem, relay_recv_sem, pass_send_sem, pass_recv_sem = scratch[43:]
     blocks = mass_ref.shape[0]
     size_x, size_y = lax.axis_size("gx"), lax.axis_size("gy")
     me_x, me_y = lax.axis_index("gx"), lax.axis_index("gy")
@@ -571,25 +572,28 @@
         ]
         row = half * padded_nodes + group * SUB
         code = codes_ref[pl.ds(pl.multiple_of(row, SUB), SUB), :]
-        shifted = code + (code >= 13).astype(jnp.int32)
-        normal = [shifted // 9 - 1, shifted // 3 % 3 - 1, shifted % 3 - 1]
-        normal = [n.astype(F32) for n in normal]
-        length = jnp.sqrt(
+        shifted = jnp.where(code >= 13, code + 1, code).astype(F32)
+        nines = jnp.floor(shifted * (1.0 / 9.0) + 0.01)
+        rest = shifted - 9.0 * nines
+        threes = jnp.floor(rest * (1.0 / 3.0) + 0.01)
+        normal = [nines - 1.0, threes - 1.0, rest - 3.0 * threes - 1.0]
+        scale = lax.rsqrt(
             normal[0] * normal[0] + normal[1] * normal[1] + normal[2] * normal[2]
         )
-        normal = [n / length for n in normal]
+        normal = [n * scale for n in normal]
         masses = [channels[0], channels[4]]
         momenta = [channels[1:4], channels[5:8]]
         gravity = [0.0, 0.0, DT * GRAVITY]
+        inverse = [1.0 / jnp.maximum(masses[f], FLOOR) for f in range(2)]
         speeds = [
-            [p / jnp.maximum(masses[f], FLOOR) + gravity[r] for r, p in enumerate(momenta[f])]
+            [p * inverse[f] + gravity[r] for r, p in enumerate(momenta[f])]
             for f in range(2)
         ]
-        both = jnp.maximum(masses[0] + masses[1], FLOOR)
+        both = 1.0 / jnp.maximum(masses[0] + masses[1], FLOOR)
         center = [
-            (momenta[0][r] + momenta[1][r]) / both + gravity[r] for r in range(3)
+            (momenta[0][r] + momenta[1][r]) * both + gravity[r] for r in range(3)
         ]
-        share = jnp.minimum(1.0, jnp.minimum(masses[0], masses[1]) / FLOOR)
+        share = jnp.minimum(1.0, jnp.minimum(masses[0], masses[1]) * (1.0 / FLOOR))
         closing = [
             share
             * jnp.maximum(
@@ -601,8 +605,9 @@
             ),
         ]
         node = group * SUB + lax.broadcasted_iota(jnp.int32, (SUB, LANES), 0)
-        x = me_x * own_x + node % n_x
-        y = me_y * own_y + node // n_x
+        layer = jnp.floor((node.astype(F32) + 0.5) * (1.0 / n_x)).astype(jnp.int32)
+        x = me_x * own_x + node - layer * n_x
+        y = me_y * own_y + layer
         inside = (x >= 1) & (x <= size_x * own_x) & (y >= 1) & (y <= size_y * own_y)
         for f, sign in ((0, -1.0), (1, 1.0)):
             for r in range(3):
@@ -679,6 +684,16 @@
         return carry
 
     lax.fori_loop(0, blocks // unroll, gather_step, 0)
+    live = slot < count_ref[0, 0]
+    even = body_ref[...] % 2 == 0
+    for v in range(4):
+        for r in range(3):
+            fields = [
+                result_ref[pl.ds(v * blocks * SUB + 4 * f + r, blocks, stride=SUB), :]
+                for f in range(2)
+            ]
+            value = jnp.where(live, jnp.where(even, fields[0], fields[1]), 0.0)
+            chosen_ref[3 * v + r] = value if v == 0 else 4.0 * value
 
     for index in range(8):
 
@@ -713,14 +728,12 @@
     count_ref,
     result_hbm,
     deform_hbm,
-    body_hbm,
     new_velocity_hbm,
     new_affine_hbm,
     new_deform_hbm,
     new_stress_hbm,
     result_ref,
     deform_ref,
-    body_ref,
     new_velocity_ref,
     new_affine_ref,
     new_deform_ref,
@@ -728,7 +741,7 @@
     in_sem,
     out_sem,
 ):
-    pairs = ((result_hbm, result_ref), (deform_hbm, deform_ref), (body_hbm, body_ref))
+    pairs = ((result_hbm, result_ref), (deform_hbm, deform_ref))
     loads = [
         pltpu.make_async_copy(source, target, in_sem.at[i])
         for i, (source, target) in enumerate(pairs)
@@ -747,22 +760,12 @@
     ]
     for load in loads:
         load.wait()
-    blocks = body_ref.shape[0]
-    slot = lax.broadcasted_iota(jnp.int32, body_ref.shape, 0)
+    slot = lax.broadcasted_iota(jnp.int32, result_ref.shape[1:], 0)
     live = slot < count_ref[0, 0]
-    even = body_ref[...] % 2 == 0
-
-    def take(v, r):
-        fields = [
-            result_ref[pl.ds(v * blocks * SUB + 4 * f + r, blocks, stride=SUB), :]
-            for f in range(2)
-        ]
-        return jnp.where(live, jnp.where(even, fields[0], fields[1]), 0.0)
-
     for r in range(3):
-        new_velocity_ref[r] = take(0, r)
+        new_velocity_ref[r] = result_ref[r]
     stores[0].start()
-    affine = [4.0 * take(1 + c, r) for r in range(3) for c in range(3)]
+    affine = [result_ref[3 + 3 * c + r] for r in range(3) for c in range(3)]
     deform = [deform_ref[i] for i in range(9)]
     moved = []
     for r in range(3):
@@ -808,7 +811,7 @@
     vmem = pl.BlockSpec(memory_space=pltpu.VMEM)
     smem = pl.BlockSpec(memory_space=pltpu.SMEM)
     hbm = pl.BlockSpec(memory_space=pltpu.HBM)
-    result_shape = jax.ShapeDtypeStruct((4 * blocks * SUB, LANES), F32)
+    result_shape = jax.ShapeDtypeStruct((12, blocks, LANES), F32)
     operands = (offset, particle_mass, velocity, affine, deform, particle_cell, body_id)
     operands = operands + (normal_code,)
     faces = [
@@ -841,6 +844,7 @@
             pltpu.VMEM((tiles[1] + 1, TILE_Z * SUB, LANES), F32),
             pltpu.VMEM((blocks, LANES, 3 * LANES), BF16),
             pltpu.VMEM((blocks, LANES, 3 * LANES), BF16),
+            pltpu.VMEM((4 * blocks * SUB, LANES), F32),
         ]
         + faces
         + faces
@@ -854,17 +858,16 @@
     return pl.pallas_call(
         particle_kernel,
         out_shape=tuple(shapes),
-        in_specs=[smem] + [hbm] * 3,
+        in_specs=[smem] + [hbm] * 2,
         out_specs=(hbm,) * 4,
         scratch_shapes=[
             pltpu.VMEM(result_shape.shape, F32),
             pltpu.VMEM(deform.shape, F32),
-            pltpu.VMEM(body_id.shape, jnp.int32),
         ]
         + [pltpu.VMEM(a.shape, F32) for a in shapes]
-        + [dma((3,)), dma((4,))],
+        + [dma((2,)), dma((4,))],
         name="particles_step",
-    )(block_count, result, deform, body_id)
+    )(block_count, result, deform)
 
 
 def solution(mesh):

time: 20.9 us -> 20.5 us (0.981)
  Pallas kernels: 19.3 us -> 18.9 us
    pallas_call x1, Pallas kernels: 17.5 us -> 17.2 us  [per_device(): pl.pallas_call(functools.partial(nodes_kernel, (n_x, n_y, padded_nodes, h...]
where the time goes in v7:
time: 20.5 us; the launch traced here: 20.2 us
  Pallas kernels  18.9 us (92%)
  between operations  1.29 us (6%)
    pallas_call x1, Pallas kernels, per_device(): pl.pallas_call(functools.partial(nodes_kernel, (n_x, n_y, padded_nodes, h...  17.2 us
    pallas_call x1, Pallas kernels, per_device(): pl.pallas_call(particle_kernel, out_shape=tuple(shapes), in_specs=[smem]...  1.75 us

profile of v7, /device:TPU:13, one launch (start us, length us, event | category | flops | bytes accessed | tf_op | source)
XLA Modules:
  0.0 20.2 jit_solution(16494552776043190335)
XLA Ops:
  1.3 17.2 %nodes_step.1.result_hbm = f32[12,24,128]{2,1,0:T(8,128)} custom-call(s32[24]{0:T(128)} %tile_ref.1, s32[1,1]{1,0:T(1,128)S(6)} %copy.14.count_ref, f32[3,24,128]{2,1,0:T(8,128)} %offset_hbm.1, f32[24,128]{1,0:T(8,128)} %mass_hbm.1, f32[3,24,128]{2,1,0:T(8,128)} %velocity_hbm.1, f32[9,24,128]{2,1,0:T(8,128)} %affine_hbm.1, f32[9,24,128]{2,1,0:T(8,128)} %deform_hbm.3, ...), custom_call_target="tpu_custom_call" | custom-call | tf_op jit(solution)/shard_map/nodes_step/pallas_call | solution.py:824
  18.5 1.7 %particles_step.1 = (f32[3,24,128]{2,1,0:T(8,128)}, f32[9,24,128]{2,1,0:T(8,128)}, f32[9,24,128]{2,1,0:T(8,128)}, f32[6,24,128]{2,1,0:T(8,128)}) custom-call(s32[1,1]{1,0:T(1,128)S(6)} %copy.14.count_ref, f32[12,24,128]{2,1,0:T(8,128)} %nodes_step.1.result_hbm, f32[9,24,128]{2,1,0:T(8,128)} %deform_hbm.3), custom_call_target="tpu_custom_call" | custom-call | tf_op jit(solution)/shard_map/particles_step/pallas_call | solution.py:858
